TPU v7x, 32 devices: a whole 2x2x4 slice. The times are simulated.
32 devices in a mesh: seq: 16 (over z, x, core), tp: 2 (over y).
Axes of the slice: x: 2, y: 2, z: 4, core: 2. Of those that a mesh axis runs over, the one named last changes fastest.
Arguments:
- noisy: bfloat16 [2, 6144, 1024], P(None, 'seq', 'tp'), may hold values from -6 to 6
- levels: int32 [2], replicated, may hold values from 0 to 999, as said below
- pairs: int32 [48, 4], P('seq'), may hold values from 0 to 47, as said below
- w_qkv: bfloat16 [3, 1024, 1024], P(None, None, 'tp'), may hold values from -4 to 4
- w_out: bfloat16 [1024, 1024], P('tp'), may hold values from -0.1875 to 0.1875
- w_up: bfloat16 [1024, 3072], P(None, 'tp'), may hold values from -0.1875 to 0.1875
- w_down: bfloat16 [3072, 1024], P('tp'), may hold values from -0.109375 to 0.109375
Outputs:
- denoised: bfloat16 [2, 6144, 1024], P(None, 'seq', 'tp')
Inputs may be any that keep to these rules, and one draw needn't show every extreme that they name: For query block b and section s, pairs[b, s] lies in the group of 3 consecutive blocks numbered g XOR (48 * 128 // (384 * 2 ** (s + 1))), where g = b // 3; at each section the query blocks of one group name each block of that group once. The samples' levels differ from one another; one sample has level 999.
All inputs are finite; a program needn't handle non-finite values.
Results may differ from a plain program's by a relative error of at most 0.017.
Values may be sent and summed in bfloat16 or wider, within the bound.
A program may use at most 192 MiB of HBM per device.

v0:
```python
import math

import jax
import jax.numpy as jnp
from jax import lax
from jax.sharding import PartitionSpec as P

D = 1024
HEADS = 16
BLOCK = 128
SECTIONS = 4


def partner(x, axis, stride):
    return lax.ppermute(x, axis, [(i, i ^ 1 << stride) for i in range(lax.axis_size(axis))])


def level_features(levels, model_width):
    half_count = model_width // 2
    index_row = jnp.arange(half_count, dtype=jnp.float32)
    freqs = jnp.exp(-math.log(10000.0) * index_row / half_count)
    angles = levels.astype(jnp.float32)[:, None] * freqs[None, :]
    return jnp.concatenate([jnp.sin(angles), jnp.cos(angles)], axis=1)


def rms_norm(values):
    return values * lax.rsqrt(jnp.mean(values * values, axis=-1, keepdims=True) + 1e-06)


def condition(gathered, level_feat):
    return (rms_norm(gathered.astype(jnp.float32)) + level_feat[:, None, :]).astype(jnp.bfloat16)


def per_device(noisy, levels, pairs, w_qkv, w_out, w_up, w_down):
    samples, tok_rows, half_width = noisy.shape
    gathered = lax.all_gather(noisy, "tp", axis=2, tiled=True)
    model_width = gathered.shape[2]
    level_feat = level_features(levels, model_width)
    normed = condition(gathered, level_feat)
    projected = jnp.einsum(
        "std,cde->cste", normed, w_qkv, preferred_element_type=jnp.float32
    ).astype(jnp.bfloat16)
    queries, keys_here, values_here = (projected[0], projected[1], projected[2])
    blocks_dev = tok_rows // BLOCK
    head_dim = D // HEADS
    local_width = w_qkv.shape[2]
    local_heads = local_width // head_dim
    axis_bits = lax.axis_size("seq").bit_length() - 1
    far_keys = []
    far_values = []
    for section_idx in range(SECTIONS):
        bit_pos = axis_bits - 1 - section_idx
        got_keys, got_values = partner((keys_here, values_here), "seq", bit_pos)
        offset = pairs[:, section_idx] % blocks_dev
        far_keys.append(
            jnp.take(got_keys.reshape(samples, blocks_dev, BLOCK, local_width), offset, axis=1)
        )
        far_values.append(
            jnp.take(got_values.reshape(samples, blocks_dev, BLOCK, local_width), offset, axis=1)
        )
    far_count = SECTIONS * BLOCK
    key_far = jnp.concatenate(far_keys, axis=2).reshape(
        samples, blocks_dev, far_count, local_heads, head_dim
    )
    value_far = jnp.concatenate(far_values, axis=2).reshape(
        samples, blocks_dev, far_count, local_heads, head_dim
    )
    query_heads = queries.reshape(samples, blocks_dev, BLOCK, local_heads, head_dim)
    key_near = keys_here.reshape(samples, tok_rows, local_heads, head_dim)
    value_near = values_here.reshape(samples, tok_rows, local_heads, head_dim)
    scale = 1.0 / math.sqrt(head_dim)
    near_scores = jnp.einsum(
        "sbqhd,skhd->sbhqk", query_heads, key_near, preferred_element_type=jnp.float32
    )
    far_scores = jnp.einsum(
        "sbqhd,sbkhd->sbhqk", query_heads, key_far, preferred_element_type=jnp.float32
    )
    scores = jnp.concatenate([near_scores, far_scores], axis=-1) * scale
    probs = jax.nn.softmax(scores, axis=-1).astype(jnp.bfloat16)
    mixed = jnp.einsum(
        "sbhqk,skhd->sbqhd", probs[..., :tok_rows], value_near, preferred_element_type=jnp.float32
    )
    mixed = mixed + jnp.einsum(
        "sbhqk,sbkhd->sbqhd", probs[..., tok_rows:], value_far, preferred_element_type=jnp.float32
    )
    mixed = mixed.astype(jnp.bfloat16).reshape(samples, tok_rows, local_width)
    attn_part = jnp.einsum("sth,hd->std", mixed, w_out, preferred_element_type=jnp.float32)
    attn_half = lax.psum_scatter(attn_part, "tp", scatter_dimension=2, tiled=True)
    middle_half = (noisy.astype(jnp.float32) + attn_half).astype(jnp.bfloat16)
    middle = lax.all_gather(middle_half, "tp", axis=2, tiled=True)
    inner = rms_norm(middle.astype(jnp.float32)).astype(jnp.bfloat16)
    hidden = jax.nn.gelu(
        jnp.einsum("std,df->stf", inner, w_up, preferred_element_type=jnp.float32), approximate=True
    ).astype(jnp.bfloat16)
    down_part = jnp.einsum("stf,fd->std", hidden, w_down, preferred_element_type=jnp.float32)
    down_half = lax.psum_scatter(
        down_part.astype(jnp.bfloat16), "tp", scatter_dimension=2, tiled=True
    ).astype(jnp.float32)
    return (middle_half.astype(jnp.float32) + down_half).astype(jnp.bfloat16)


def solution(mesh):
    in_specs = (
        P(None, "seq", "tp"),
        P(),
        P("seq", None),
        P(None, None, "tp"),
        P("tp", None),
        P(None, "tp"),
        P("tp", None),
    )
    out_specs = P(None, "seq", "tp")
    return jax.shard_map(
        per_device, mesh=mesh, in_specs=in_specs, out_specs=out_specs, check_vma=False
    )
```

profile of v0, /device:TPU:0, one launch (start us, length us, event | category | flops | bytes accessed | tf_op | source)
XLA Modules:
  0.0 315.8 jit_solution(4933473980621709197)
XLA Ops:
  9.4 29.5 %all-gather.3.cloned.1.call-done = bf16[2,384,1024]{2,1,0:T(8,128)(2,1)} async-done(((bf16[2,384,512]{2,1,0:T(8,128)(2,1)}), bf16[2,384,1024]{2,1,0:T(8,128)(2,1)}) %all-gather.3.cloned.1.call-update) | async-done | bytes 1572880 | tf_op jit(solution)/shard_map/all_gather | solution.py:36
  40.7 4.4 %convert_bitcast_fusion = bf16[3,2,384,512]{3,2,0,1:T(8,128)(2,1)S(1)} fusion(bf16[3,1024,512]{2,1,0:T(8,128)(2,1)S(1)} %copy-done, bf16[2,384,1024]{2,1,0:T(8,128)(2,1)} %all-gather.3.cloned.1.call-done, f32[2,1024]{1,0:T(2,128)S(1)} %pad_maximum_fusion.2, f32[2,384]{1,0:T(2,128)S(1)} %add_rsqrt_fusion.1), kind=kOutput, calls=%fused_computation.46 | convolution fusion | flops 2420244480 | bytes 7089152 | tf_op jit(solution)/shard_map/std,cde->cste/dot_general | solution.py:40
  52.8 14.4 %collective-permute-done.6 = bf16[2,384,512]{2,1,0:T(8,128)(2,1)} collective-permute-done((bf16[2,384,512]{2,1,0:T(8,128)(2,1)}, bf16[2,384,512]{2,1,0:T(8,128)(2,1)}, u32[]{:S(2)}, u32[]{:S(2)}) %collective-permute-start.6) | collective-permute-done | bytes 786464 | tf_op jit(solution)/shard_map/ppermute | solution.py:15
  73.3 5.1 %convolution_bitcast_fusion = f32[2,3,8,128,384]{3,4,1,2,0:T(8,128)} fusion(bf16[2,384,8,64,1]{1,3,4,2,0:T(8,128)(2,1)S(1)} %bitcast.85, bf16[2,3,128,8,64]{2,1,4,3,0:T(4,128)(2,1)S(1)} %reshape_squeeze.11), kind=kOutput, calls=%fused_computation.31 | convolution fusion | flops 301989888 | bytes 11010048 | tf_op jit(solution)/shard_map/sbqhd,skhd->sbhqk/dot_general | solution.py:72
  78.4 9.6 %copy.23 = f32[2,3,8,128,384]{4,3,2,1,0:T(8,128)} copy(f32[2,3,8,128,384]{3,4,1,2,0:T(8,128)} %convolution_bitcast_fusion) | data formatting | bytes 18874368 | tf_op jit(solution)/shard_map/sbqhd,skhd->sbhqk/transpose | solution.py:72
  91.5 2.7 gather_fusion.6
  94.1 2.6 gather_fusion.2
  96.8 2.6 gather_fusion.5
  99.4 19.4 %collective-permute-done.1 = bf16[2,384,512]{2,1,0:T(8,128)(2,1)} collective-permute-done((bf16[2,384,512]{2,1,0:T(8,128)(2,1)}, bf16[2,384,512]{2,1,0:T(8,128)(2,1)}, u32[]{:S(2)}, u32[]{:S(2)}) %collective-permute-start.1) | collective-permute-done | bytes 786464 | tf_op jit(solution)/shard_map/ppermute | solution.py:15
  118.8 2.6 gather_fusion.1
  121.4 2.6 gather_fusion.4
  124.1 2.6 gather_fusion
  130.4 2.9 pad_maximum_fusion
  133.4 3.3 %copy.21 = bf16[2,3,512,512]{2,3,1,0:T(8,128)(2,1)S(1)} copy(bf16[2,3,512,512]{3,2,0,1:T(8,128)(2,1)} %get-tuple-element.35) | data formatting | bytes 6291456 | tf_op jit(solution)/shard_map/concatenate | solution.py:62
  136.7 4.7 %copy.25 = bf16[2,3,512,512]{2,3,1,0:T(8,128)(2,1)} copy(bf16[2,3,512,512]{3,2,0,1:T(8,128)(2,1)} %get-tuple-element.36) | data formatting | bytes 6291456 | tf_op jit(solution)/shard_map/concatenate | solution.py:65
  141.4 7.6 %fusion.47 = f32[2,3,8,128,512]{4,3,2,1,0:T(8,128)} fusion(bf16[2,3,512,8,64]{2,4,3,1,0:T(8,128)(2,1)S(1)} %bitcast.83, bf16[2,3,128,8,64]{2,1,4,3,0:T(4,128)(2,1)} %copy-done.2), kind=kOutput, calls=%fused_computation.58 | convolution fusion | flops 402653184 | bytes 16515072 | tf_op jit(solution)/shard_map/sbqhd,sbkhd->sbhqk/dot_general | solution.py:75
  148.9 23.8 %fusion.15 = (f32[2,3,8,128]{3,2,1,0:T(8,128)S(1)}, f32[2,3,8,128,896]{4,3,2,1,0:T(8,128)}) fusion(f32[2,3,8,128,512]{4,3,2,1,0:T(8,128)} %fusion.47, f32[2,3,8,128,384]{4,3,2,1,0:T(8,128)} %copy.23), kind=kOutput, calls=%fused_computation.32 | output fusion | flops 33031040 | bytes 44064768 | tf_op jit(solution)/shard_map/sub | solution.py:79
  172.7 15.0 %divide_convert_fusion = bf16[2,3,8,128,896]{4,3,2,1,0:T(8,128)(2,1)S(1)} fusion(f32[2,3,8,128]{3,2,1,0:T(8,128)S(1)} %get-tuple-element.33, f32[2,3,8,128,896]{4,3,2,1,0:T(8,128)} %get-tuple-element.34, f32[2,3,8,128,512]{4,3,2,1,0:T(8,128)} %fusion.47, f32[2,3,8,128,384]{4,3,2,1,0:T(8,128)} %copy.23), kind=kLoop, calls=%fused_computation.10 | loop fusion | flops 27525120 | bytes 55074816 | tf_op jit(solution)/shard_map/convert_element_type | solution.py:79
  187.7 2.6 fusion.3
  193.6 3.9 %fusion.45 = f32[2,384,1024]{2,1,0:T(8,128)} fusion(bf16[2,384,512]{1,2,0:T(8,128)(2,1)S(1)} %reshape.178, bf16[512,1024]{1,0:T(8,128)(2,1)} %param.13), kind=kOutput, calls=%fused_computation.56 | convolution fusion | flops 805306368 | bytes 4980736 | tf_op jit(solution)/shard_map/sth,hd->std/dot_general | solution.py:87
  197.5 41.6 %reduce-scatter.3.cloned.1.call-done = f32[2,384,512]{2,1,0:T(8,128)} async-done(((f32[2,384,1024]{2,1,0:T(8,128)}), f32[2,384,512]{2,1,0:T(8,128)}) %reduce-scatter.3.cloned.1.call-update) | async-done | bytes 1572880 | tf_op jit(solution)/shard_map/reduce_scatter | solution.py:88
  241.7 27.3 %all-gather.5.cloned.1.call-done = bf16[2,384,1024]{2,1,0:T(8,128)(2,1)} async-done(((bf16[2,384,512]{2,1,0:T(8,128)(2,1)}), bf16[2,384,1024]{2,1,0:T(8,128)(2,1)}) %all-gather.5.cloned.1.call-update) | async-done | bytes 1572880 | tf_op jit(solution)/shard_map/all_gather | solution.py:90
  270.8 9.7 %fusion.29 = bf16[2,384,1024]{2,1,0:T(8,128)(2,1)} fusion(bf16[1536,1024]{1,0:T(8,128)(2,1)} %param.15, bf16[1024,1536]{1,0:T(8,128)(2,1)} %param.14, bf16[2,384,1024]{2,1,0:T(8,128)(2,1)} %all-gather.5.cloned.1.call-done, f32[2,384]{1,0:T(2,128)S(1)} %add_rsqrt_fusion), kind=kOutput, calls=%fused_computation.47 | convolution fusion | flops 4845600768 | bytes 9440256 | tf_op jit(solution)/shard_map/stf,fd->std/dot_general | solution.py:95
  280.6 26.2 %reduce-scatter.5.cloned.1.call-done = bf16[2,384,512]{2,1,0:T(8,128)(2,1)} async-done(((bf16[2,384,1024]{2,1,0:T(8,128)(2,1)}), bf16[2,384,512]{2,1,0:T(8,128)(2,1)}) %reduce-scatter.5.cloned.1.call-update) | async-done | bytes 786448 | tf_op jit(solution)/shard_map/reduce_scatter | solution.py:96
  (71 shorter events, 35.7 us)
Async XLA Ops:
  6.5 34.1 %copy-start = (bf16[3,1024,512]{2,1,0:T(8,128)(2,1)S(1)}, bf16[3,1024,512]{2,1,0:T(8,128)(2,1)}, u32[]{:S(2)}) copy-start(bf16[3,1024,512]{2,1,0:T(8,128)(2,1)} %param.12) | copy-start | bytes 9437188
  6.5 32.3 %all-gather.3.cloned.1.call-start = ((), (), s32[]{:S(2)}) async-start(), calls=%async_computation.2 | async-start | bytes 2359296 | tf_op jit(solution)/shard_map/all_gather | solution.py:36
  7.3 231.8 %reduce-scatter.3.cloned.1.call-start = ((), (), s32[]{:S(2)}) async-start(), calls=%async_computation.3 | async-start | bytes 4718592 | tf_op jit(solution)/shard_map/reduce_scatter | solution.py:88
  46.5 5.7 %collective-permute-start.7 = (bf16[2,384,512]{2,1,0:T(8,128)(2,1)}, bf16[2,384,512]{2,1,0:T(8,128)(2,1)}, u32[]{:S(2)}, u32[]{:S(2)}) collective-permute-start(bf16[2,384,512]{2,1,0:T(8,128)(2,1)} %get-tuple-element.19), channel_id=1, source_target_pairs={{0,2},{2,0},{4,6},{6,4},{8,10},{10,8},{12,14},{14,12},{16,18},{18,... | collective-permute-start | bytes 2359304 | tf_op jit(solution)/shard_map/ppermute | solution.py:15
  46.5 20.7 %collective-permute-start.6 = (bf16[2,384,512]{2,1,0:T(8,128)(2,1)}, bf16[2,384,512]{2,1,0:T(8,128)(2,1)}, u32[]{:S(2)}, u32[]{:S(2)}) collective-permute-start(bf16[2,384,512]{2,1,0:T(8,128)(2,1)} %get-tuple-element.19), channel_id=1, source_target_pairs={{0,4},{2,6},{4,0},{6,2},{8,12},{10,14},{12,8},{14,10},{16,20},{18,... | collective-permute-start | bytes 2359304 | tf_op jit(solution)/shard_map/ppermute | solution.py:15
  48.0 20.7 %collective-permute-start.3 = (bf16[2,384,512]{2,1,0:T(8,128)(2,1)}, bf16[2,384,512]{2,1,0:T(8,128)(2,1)}, u32[]{:S(2)}, u32[]{:S(2)}) collective-permute-start(bf16[2,384,512]{2,1,0:T(8,128)(2,1)} %get-tuple-element.20), channel_id=1, source_target_pairs={{0,2},{2,0},{4,6},{6,4},{8,10},{10,8},{12,14},{14,12},{16,18},{18,... | collective-permute-start | bytes 2359304 | tf_op jit(solution)/shard_map/ppermute | solution.py:15
  48.3 48.5 %collective-permute-start.5 = (bf16[2,384,512]{2,1,0:T(8,128)(2,1)}, bf16[2,384,512]{2,1,0:T(8,128)(2,1)}, u32[]{:S(2)}, u32[]{:S(2)}) collective-permute-start(bf16[2,384,512]{2,1,0:T(8,128)(2,1)} %get-tuple-element.19), channel_id=1, source_target_pairs={{0,8},{2,10},{4,12},{6,14},{8,0},{10,2},{12,4},{14,6},{16,24},{18,... | collective-permute-start | bytes 2359304 | tf_op jit(solution)/shard_map/ppermute | solution.py:15
  49.9 71.6 %collective-permute-start.4 = (bf16[2,384,512]{2,1,0:T(8,128)(2,1)}, bf16[2,384,512]{2,1,0:T(8,128)(2,1)}, u32[]{:S(2)}, u32[]{:S(2)}) collective-permute-start(bf16[2,384,512]{2,1,0:T(8,128)(2,1)} %get-tuple-element.19), channel_id=1, source_target_pairs={{0,16},{2,18},{4,20},{6,22},{8,24},{10,26},{12,28},{14,30},{16,0},... | collective-permute-start | bytes 2359304 | tf_op jit(solution)/shard_map/ppermute | solution.py:15
  52.3 41.9 %collective-permute-start.2 = (bf16[2,384,512]{2,1,0:T(8,128)(2,1)}, bf16[2,384,512]{2,1,0:T(8,128)(2,1)}, u32[]{:S(2)}, u32[]{:S(2)}) collective-permute-start(bf16[2,384,512]{2,1,0:T(8,128)(2,1)} %get-tuple-element.20), channel_id=1, source_target_pairs={{0,4},{2,6},{4,0},{6,2},{8,12},{10,14},{12,8},{14,10},{16,20},{18,... | collective-permute-start | bytes 2359304 | tf_op jit(solution)/shard_map/ppermute | solution.py:15
  67.2 51.6 %collective-permute-start.1 = (bf16[2,384,512]{2,1,0:T(8,128)(2,1)}, bf16[2,384,512]{2,1,0:T(8,128)(2,1)}, u32[]{:S(2)}, u32[]{:S(2)}) collective-permute-start(bf16[2,384,512]{2,1,0:T(8,128)(2,1)} %get-tuple-element.20), channel_id=1, source_target_pairs={{0,8},{2,10},{4,12},{6,14},{8,0},{10,2},{12,4},{14,6},{16,24},{18,... | collective-permute-start | bytes 2359304 | tf_op jit(solution)/shard_map/ppermute | solution.py:15
  68.7 55.4 %collective-permute-start = (bf16[2,384,512]{2,1,0:T(8,128)(2,1)}, bf16[2,384,512]{2,1,0:T(8,128)(2,1)}, u32[]{:S(2)}, u32[]{:S(2)}) collective-permute-start(bf16[2,384,512]{2,1,0:T(8,128)(2,1)} %get-tuple-element.20), channel_id=1, source_target_pairs={{0,16},{2,18},{4,20},{6,22},{8,24},{10,26},{12,28},{14,30},{16,0},... | collective-permute-start | bytes 2359304 | tf_op jit(solution)/shard_map/ppermute | solution.py:15
  72.9 5.4 %copy-start.2 = (bf16[2,3,128,8,64]{2,1,4,3,0:T(4,128)(2,1)}, bf16[2,3,128,8,64]{2,1,4,3,0:T(4,128)(2,1)S(1)}, u32[]{:S(2)}) copy-start(bf16[2,3,128,8,64]{2,1,4,3,0:T(4,128)(2,1)S(1)} %reshape_squeeze.11) | copy-start | bytes 2359300
  126.7 3.5 %copy-start.5 = (bf16[3,2,128,512]{3,2,1,0:T(8,128)(2,1)S(1)}, bf16[3,2,128,512]{3,2,1,0:T(8,128)(2,1)}, u32[]{:S(2)}) copy-start(bf16[3,2,128,512]{3,2,1,0:T(8,128)(2,1)} %gather_fusion.4) | copy-start | bytes 2359300
  126.7 3.5 %copy-start.6 = (bf16[3,2,128,512]{3,2,1,0:T(8,128)(2,1)S(1)}, bf16[3,2,128,512]{3,2,1,0:T(8,128)(2,1)}, u32[]{:S(2)}) copy-start(bf16[3,2,128,512]{3,2,1,0:T(8,128)(2,1)} %gather_fusion) | copy-start | bytes 2359300
  172.7 15.0 %copy-start.3 = (bf16[2,3,512,512]{2,3,1,0:T(8,128)(2,1)S(1)}, bf16[2,3,512,512]{2,3,1,0:T(8,128)(2,1)}, u32[]{:S(2)}) copy-start(bf16[2,3,512,512]{2,3,1,0:T(8,128)(2,1)} %copy.25) | copy-start | bytes 9437188
  187.7 2.6 copy-start.7
  192.8 46.2 %copy-start.4 = (bf16[2,384,512]{2,1,0:T(8,128)(2,1)S(1)}, bf16[2,384,512]{2,1,0:T(8,128)(2,1)}, u32[]{:S(2)}) copy-start(bf16[2,384,512]{2,1,0:T(8,128)(2,1)} %param.9) | copy-start | bytes 2359300
  197.5 71.6 %all-gather.5.cloned.1.call-start = ((), (), s32[]{:S(2)}) async-start(), calls=%async_computation.4 | async-start | bytes 2359296 | tf_op jit(solution)/shard_map/all_gather | solution.py:90
  241.7 65.2 %reduce-scatter.5.cloned.1.call-start = ((), (), s32[]{:S(2)}) async-start(), calls=%async_computation.5 | async-start | bytes 2359296 | tf_op jit(solution)/shard_map/reduce_scatter | solution.py:96
  270.8 38.5 %copy-start.1 = (bf16[3,1024,512]{2,1,0:T(8,128)(2,1)S(1)}, bf16[3,1024,512]{2,1,0:T(8,128)(2,1)}, u32[]{:S(2)}) copy-start(bf16[3,1024,512]{2,1,0:T(8,128)(2,1)} %param.12) | copy-start | bytes 9437188
Sparse Core Ops, SparseCore 0:
  8.9 29.8 all-gather.2
  197.6 41.4 reduce-scatter.2
  241.8 27.2 all-gather.4
  280.7 26.0 reduce-scatter.4
where the time goes:
time: 317 us; the launch traced here: 316 us
  waiting for transfers between devices  159 us (50%)
  other arithmetic  56.1 us (18%)
  local copies, waits for them, and re-layouts  42 us (13%)
  matrix products  35 us (11%)
  between operations  13.4 us (4%)
  starting transfers between devices  10.2 us (3%)
    reduce_scatter x1, waiting for transfers between devices, per_device(): lax.psum_scatter(attn_part, 'tp', scatter_dimension=2, tiled=True)  41.6 us
    ppermute x8, waiting for transfers between devices, partner(): lax.ppermute(x, axis, [(i, i ^ 1 << stride) for i in range(lax.axis_size(...  33.7 us
    all_gather x1, waiting for transfers between devices, per_device(): gathered = lax.all_gather(noisy, 'tp', axis=2, tiled=True)  29.5 us
    all_gather x1, waiting for transfers between devices, per_device(): middle = lax.all_gather(middle_half, 'tp', axis=2, tiled=True)  27.3 us
    reduce_scatter x1, waiting for transfers between devices, per_device(): lax.psum_scatter(down_part.astype(jnp.bfloat16), 'tp', scatter_dimension=...  26.2 us
    sub x1, other arithmetic, per_device(): probs = jax.nn.softmax(scores, axis=-1).astype(jnp.bfloat16)  23.8 us
    convert_element_type x1, other arithmetic, per_device(): probs = jax.nn.softmax(scores, axis=-1).astype(jnp.bfloat16)  15 us
    ppermute x8, starting transfers between devices, partner(): lax.ppermute(x, axis, [(i, i ^ 1 << stride) for i in range(lax.axis_size(...  10.1 us
  transfers between devices with their start and end apart: 12, of which 6 were waited for; matrix products, arithmetic and copies ran while one was open for 11% of the time, Pallas kernels for 0%

commit v1 on v0

v1 whole, which is shorter than its diff:
```python
import functools
import math

import jax
import jax.numpy as jnp
from jax import lax
from jax.experimental import pallas as pl
from jax.experimental.pallas import tpu as pltpu
from jax.sharding import PartitionSpec as P

HEADS = 16
BLOCK = 128
LANES = 128
RAW_SECTIONS = (0,)


def partner(x, axis, bit):
    return lax.ppermute(x, axis, [(i, i ^ 1 << bit) for i in range(lax.axis_size(axis))])


def both_halves(own, other, low):
    first = jnp.where(low, own, other)
    second = jnp.where(low, other, own)
    return jnp.concatenate([first, second], axis=-1)


def level_features(levels, model_width):
    half_count = model_width // 2
    index_row = jnp.arange(half_count, dtype=jnp.float32)
    freqs = jnp.exp(-math.log(10000.0) * index_row / half_count)
    angles = levels.astype(jnp.float32)[:, None] * freqs[None, :]
    return jnp.concatenate([jnp.sin(angles), jnp.cos(angles)], axis=1)


def rms_norm(values):
    return values * lax.rsqrt(jnp.mean(values * values, axis=-1, keepdims=True) + 1e-06)


def attention_kernel(sections, head_dim, offs, q_ref, near_ref, *rest):
    far_refs, out_ref = rest[:sections], rest[sections]
    rows = q_ref.shape[0]
    lane = lax.broadcasted_iota(jnp.int32, (BLOCK, LANES), 1)
    low = lane < head_dim
    scale = 1.0 / math.sqrt(head_dim)
    for b in range(rows // BLOCK):
        q = q_ref[b * BLOCK : (b + 1) * BLOCK, :].astype(jnp.float32) * scale
        q2 = jnp.concatenate([jnp.where(low, q, 0.0), jnp.where(low, 0.0, q)], axis=0)
        q2 = q2.astype(jnp.bfloat16)
        keys, values = [near_ref[0]], [near_ref[1]]
        for s in range(sections):
            at = pl.ds(pl.multiple_of(offs[b, s] * BLOCK, BLOCK), BLOCK)
            keys.append(far_refs[s][0, at, :])
            values.append(far_refs[s][1, at, :])
        keys = jnp.concatenate(keys, axis=0)
        values = jnp.concatenate(values, axis=0)
        scores = lax.dot_general(
            q2, keys, (((1,), (1,)), ((), ())), preferred_element_type=jnp.float32
        )
        top = jnp.max(scores, axis=-1, keepdims=True)
        probs = jnp.exp(scores - top)
        total = jnp.sum(probs, axis=-1, keepdims=True)
        mixed = jnp.dot(probs.astype(jnp.bfloat16), values, preferred_element_type=jnp.float32)
        mixed = mixed / total
        out_ref[b * BLOCK : (b + 1) * BLOCK, :] = jnp.where(
            low, mixed[:BLOCK], mixed[BLOCK:]
        ).astype(out_ref.dtype)


def attention(offsets, q, near, fars):
    rows, width = q.shape
    sections = len(fars)
    head_dim = 64
    key_count = rows + sections * BLOCK
    kv_spec = pl.BlockSpec((2, rows, LANES), lambda h, offs: (0, 0, h))
    row_spec = pl.BlockSpec((rows, LANES), lambda h, offs: (0, h))
    return pl.pallas_call(
        functools.partial(attention_kernel, sections, head_dim),
        out_shape=jax.ShapeDtypeStruct((rows, width), jnp.bfloat16),
        grid_spec=pltpu.PrefetchScalarGridSpec(
            num_scalar_prefetch=1,
            grid=(width // LANES,),
            in_specs=[row_spec] + [kv_spec] * (1 + sections),
            out_specs=row_spec,
        ),
        compiler_params=pltpu.CompilerParams(vmem_limit_bytes=24 * 2**20),
        cost_estimate=pl.CostEstimate(
            flops=8 * rows * key_count * width,
            bytes_accessed=2 * rows * width * (2 + 2 * (1 + sections)),
            transcendentals=rows * key_count * width // head_dim,
        ),
        name="attention",
    )(offsets, q, near, *fars)


def per_device(noisy, levels, pairs, w_qkv, w_out, w_up, w_down):
    samples, tok_rows, half_width = noisy.shape
    sections = pairs.shape[1]
    model_width = 2 * half_width
    blocks_dev = tok_rows // BLOCK
    axis_bits = lax.axis_size("seq").bit_length() - 1
    me = lax.axis_index("tp")
    low = me == 0
    bit_of = [axis_bits - 1 - s for s in range(sections)]
    offsets = (pairs % blocks_dev).astype(jnp.int32)
    level_feat = level_features(levels, model_width)
    w_q, w_kv = w_qkv[0], w_qkv[1:]

    own = [noisy[s] for s in range(samples)]
    other = [partner(x, "tp", 0) for x in own]
    raw = [{c: partner(x, "seq", bit_of[c]) for c in RAW_SECTIONS} for x in own]
    raw_other = [{c: partner(x, "tp", 0) for c, x in r.items()} for r in raw]
    w_out_other = partner(w_out, "tp", 0)

    def condition(full, s):
        return (rms_norm(full.astype(jnp.float32)) + level_feat[s]).astype(jnp.bfloat16)

    def keys_values(normed):
        return jnp.einsum(
            "td,cde->cte", normed, w_kv, preferred_element_type=jnp.float32
        ).astype(jnp.bfloat16)

    fulls, queries, nears, fars = [], [], [], []
    for s in range(samples):
        full = both_halves(own[s], other[s], low)
        normed = condition(full, s)
        near = keys_values(normed)
        far = {
            c: partner(near, "seq", bit_of[c]) for c in range(sections) if c not in RAW_SECTIONS
        }
        query = jnp.dot(normed, w_q, preferred_element_type=jnp.float32).astype(jnp.bfloat16)
        fulls.append(full)
        nears.append(near)
        fars.append(far)
        queries.append(query)
    for s in range(samples):
        for c in RAW_SECTIONS:
            far_full = both_halves(raw[s][c], raw_other[s][c], low)
            fars[s][c] = keys_values(condition(far_full, s))

    w_out_full = jnp.concatenate(
        [jnp.where(low, w_out, w_out_other), jnp.where(low, w_out_other, w_out)], axis=0
    )
    w_mine = lax.dynamic_slice_in_dim(w_down, me * half_width, half_width, 1)
    w_theirs = lax.dynamic_slice_in_dim(w_down, (1 - me) * half_width, half_width, 1)
    outs = []
    for s in range(samples):
        mixed = attention(offsets, queries[s], nears[s], [fars[s][c] for c in range(sections)])
        mixed_full = both_halves(mixed, partner(mixed, "tp", 0), low)
        attn = jnp.dot(mixed_full, w_out_full, preferred_element_type=jnp.float32)
        middle = (fulls[s].astype(jnp.float32) + attn).astype(jnp.bfloat16)
        inner = rms_norm(middle.astype(jnp.float32)).astype(jnp.bfloat16)
        hidden = jax.nn.gelu(
            jnp.dot(inner, w_up, preferred_element_type=jnp.float32), approximate=True
        ).astype(jnp.bfloat16)
        theirs = jnp.dot(hidden, w_theirs, preferred_element_type=jnp.float32)
        got = partner(theirs.astype(jnp.bfloat16), "tp", 0)
        mine = jnp.dot(hidden, w_mine, preferred_element_type=jnp.float32)
        middle_half = jnp.where(low, middle[:, :half_width], middle[:, half_width:])
        outs.append(
            (middle_half.astype(jnp.float32) + mine + got.astype(jnp.float32)).astype(jnp.bfloat16)
        )
    return jnp.stack(outs, axis=0)


def solution(mesh):
    in_specs = (
        P(None, "seq", "tp"),
        P(),
        P("seq", None),
        P(None, None, "tp"),
        P("tp", None),
        P(None, "tp"),
        P("tp", None),
    )
    out_specs = P(None, "seq", "tp")
    return jax.shard_map(
        per_device, mesh=mesh, in_specs=in_specs, out_specs=out_specs, check_vma=False
    )
```

time: 317 us -> 130 us (0.41)
  waiting for transfers between devices: 159 us -> 63 us
  other arithmetic: 56.1 us -> 6.55 us
  local copies, waits for them, and re-layouts: 42 us -> 2.66 us
  matrix products: 35 us -> 18.7 us
  Pallas kernels: 0 us -> 15.8 us
  between operations: 13.4 us -> 0.28 us
  starting transfers between devices: 10.2 us -> 22.9 us
    reduce_scatter x2 -> x0, waiting for transfers between devices: 67.8 us -> none  [the longest x1 41.6 us: per_device(): lax.psum_scatter(attn_part, 'tp', scatter_dimension=2, tiled=True)]
    all_gather x2 -> x0, waiting for transfers between devices: 56.8 us -> none  [the longest x1 29.5 us: per_device(): gathered = lax.all_gather(noisy, 'tp', axis=2, tiled=True)]
    ppermute x8 -> x17, waiting for transfers between devices: 33.7 us -> 63 us  [partner(): lax.ppermute(x, axis, [(i, i ^ 1 << bit) for i in range(lax.axis_size(axi...]
    sub x1 -> x0, other arithmetic: 23.8 us -> none  [per_device(): probs = jax.nn.softmax(scores, axis=-1).astype(jnp.bfloat16)]
    convert_element_type x3 -> x0, other arithmetic: 20 us -> none  [the longest x1 15 us: per_device(): probs = jax.nn.softmax(scores, axis=-1).astype(jnp.bfloat16)]
    gather x8 -> x0, local copies, waits for them, and re-layouts: 19.3 us -> none  [the longest x4 9.66 us: per_device(): jnp.take(got_keys.reshape(samples, blocks_dev, BLOCK, local_width), offse...]
    dot_general x7 -> x14, matrix products: 35 us -> 18.7 us  [the longest x2 4.53 us: per_device(): mine = jnp.dot(hidden, w_mine, preferred_element_type=jnp.float32)]
    pallas_call x0 -> x2, Pallas kernels: none -> 15.8 us  [attention(): pl.pallas_call(functools.partial(attention_kernel, sections, head_dim), o...]
  transfers between devices with their start and end apart: 12 -> 17, of which waited for: 6 -> 11; matrix products, arithmetic and copies ran while one was open for 11% -> 14% of each run, Pallas kernels for 0% -> 12%
where the time goes in v1:
time: 130 us
  waiting for transfers between devices  63 us (48%)
  starting transfers between devices  22.9 us (18%)
  matrix products  18.7 us (14%)
  Pallas kernels  15.8 us (12%)
  other arithmetic  6.55 us (5%)
  local copies, waits for them, and re-layouts  2.66 us (2%)
    ppermute x17, waiting for transfers between devices, partner(): lax.ppermute(x, axis, [(i, i ^ 1 << bit) for i in range(lax.axis_size(axi...  63 us
    ppermute x17, starting transfers between devices, partner(): lax.ppermute(x, axis, [(i, i ^ 1 << bit) for i in range(lax.axis_size(axi...  22.9 us
    pallas_call x2, Pallas kernels, attention(): pl.pallas_call(functools.partial(attention_kernel, sections, head_dim), o...  15.8 us
    dot_general x2, matrix products, per_device(): mine = jnp.dot(hidden, w_mine, preferred_element_type=jnp.float32)  4.53 us
    dot_general x4, matrix products, keys_values(): jnp.einsum('td,cde->cte', normed, w_kv, preferred_element_type=jnp.float32)  4.14 us
    dot_general x2, matrix products, per_device(): jnp.dot(inner, w_up, preferred_element_type=jnp.float32)  3.48 us
    dot_general x2, matrix products, per_device(): theirs = jnp.dot(hidden, w_theirs, preferred_element_type=jnp.float32)  3.07 us
    select_n x5, other arithmetic, both_halves(): first = jnp.where(low, own, other)  2.77 us
  transfers between devices with their start and end apart: 17, of which 11 were waited for; matrix products, arithmetic and copies ran while one was open for 14% of the time, Pallas kernels for 12%

profile of v1, /device:TPU:0, one launch (start us, length us, event | category | flops | bytes accessed | tf_op | source)
XLA Modules:
  0.0 129.9 jit_solution(16177438325439938181)
XLA Ops:
  0.0 2.2 %slice_bitcast_fusion.1 = (bf16[384,512]{1,0:T(8,128)(2,1)}, bf16[384,512]{1,0:T(8,128)(2,1)}) fusion(bf16[2,384,512]{2,1,0:T(8,128)(2,1)} %param.7), kind=kLoop, calls=%fused_computation.111 | loop fusion | bytes 1572864 | tf_op jit(solution)/shard_map/squeeze | solution.py:108
  2.2 4.0 %collective-permute-start.1 = (bf16[384,512]{1,0:T(8,128)(2,1)}, bf16[384,512]{1,0:T(8,128)(2,1)}, u32[]{:S(2)}, u32[]{:S(2)}) collective-permute-start(bf16[384,512]{1,0:T(8,128)(2,1)} %get-tuple-element.17), channel_id=1, source_target_pairs={{0,16},{2,18},{4,20},{6,22},{8,24},{10,26},{12,28},{14,30},{16,0},... | collective-permute-start | bytes 1179656 | tf_op jit(solution)/shard_map/ppermute | solution.py:18
  8.3 1.9 %collective-permute-start.7 = (bf16[512,1024]{1,0:T(8,128)(2,1)}, bf16[512,1024]{1,0:T(8,128)(2,1)}, u32[]{:S(2)}, u32[]{:S(2)}) collective-permute-start(bf16[512,1024]{1,0:T(8,128)(2,1)} %param.11), channel_id=1, source_target_pairs={{0,1},{1,0},{2,3},{3,2},{4,5},{5,4},{6,7},{7,6},{8,9},{9,8},{10,11... | collective-permute-start | bytes 3145736 | tf_op jit(solution)/shard_map/ppermute | solution.py:18
  10.4 8.2 %collective-permute-done = bf16[384,512]{1,0:T(8,128)(2,1)} collective-permute-done((bf16[384,512]{1,0:T(8,128)(2,1)}, bf16[384,512]{1,0:T(8,128)(2,1)}, u32[]{:S(2)}, u32[]{:S(2)}) %collective-permute-start) | collective-permute-done | bytes 393248 | tf_op jit(solution)/shard_map/ppermute | solution.py:18
  18.6 8.4 %collective-permute-done.9 = bf16[384,512]{1,0:T(8,128)(2,1)} collective-permute-done((bf16[384,512]{1,0:T(8,128)(2,1)}, bf16[384,512]{1,0:T(8,128)(2,1)}, u32[]{:S(2)}, u32[]{:S(2)}) %collective-permute-start.9) | collective-permute-done | bytes 393248 | tf_op jit(solution)/shard_map/ppermute | solution.py:18
  30.0 3.3 %collective-permute-done.1 = bf16[384,512]{1,0:T(8,128)(2,1)} collective-permute-done((bf16[384,512]{1,0:T(8,128)(2,1)}, bf16[384,512]{1,0:T(8,128)(2,1)}, u32[]{:S(2)}, u32[]{:S(2)}) %collective-permute-start.1) | collective-permute-done | bytes 393248 | tf_op jit(solution)/shard_map/ppermute | solution.py:18
  33.4 1.9 %collective-permute-start.2 = (bf16[384,512]{1,0:T(8,128)(2,1)}, bf16[384,512]{1,0:T(8,128)(2,1)S(1)}, u32[]{:S(2)}, u32[]{:S(2)}) collective-permute-start(bf16[384,512]{1,0:T(8,128)(2,1)} %collective-permute-done.1), channel_id=1, source_target_pairs={{0,1},{1,0},{2,3},{3,2},{4,5},{5,4},{6,7},{7,6},{8,9},{9,8},{10,11... | collective-permute-start | bytes 1179656 | tf_op jit(solution)/shard_map/ppermute | solution.py:18
  36.3 4.6 %collective-permute-done.10 = bf16[384,512]{1,0:T(8,128)(2,1)S(1)} collective-permute-done((bf16[384,512]{1,0:T(8,128)(2,1)}, bf16[384,512]{1,0:T(8,128)(2,1)S(1)}, u32[]{:S(2)}, u32[]{:S(2)}) %collective-permute-start.10) | collective-permute-done | bytes 393248 | tf_op jit(solution)/shard_map/ppermute | solution.py:18
  45.3 12.5 %collective-permute-done.2 = bf16[384,512]{1,0:T(8,128)(2,1)S(1)} collective-permute-done((bf16[384,512]{1,0:T(8,128)(2,1)}, bf16[384,512]{1,0:T(8,128)(2,1)S(1)}, u32[]{:S(2)}, u32[]{:S(2)}) %collective-permute-start.2) | collective-permute-done | bytes 393248 | tf_op jit(solution)/shard_map/ppermute | solution.py:18
  60.7 4.1 %collective-permute-done.11 = bf16[384,512]{1,0:T(8,128)(2,1)S(1)} collective-permute-done((bf16[384,512]{1,0:T(8,128)(2,1)S(1)}, bf16[384,512]{1,0:T(8,128)(2,1)S(1)}, u32[]{:S(2)}, u32[]{:S(2)}) %collective-permute-start.11) | collective-permute-done | bytes 393248 | tf_op jit(solution)/shard_map/ppermute | solution.py:18
  70.4 7.9 %collective-permute-done.12.rest_1_ = bf16[2,384,512]{2,1,0:T(8,128)(2,1)S(1)} collective-permute-done((bf16[2,384,512]{2,1,0:T(8,128)(2,1)S(1)}, bf16[2,384,512]{2,1,0:T(8,128)(2,1)S(1)}, u32[]{:S(2)}, u32[]{:S(2)}) %collective-permute-start.12) | collective-permute-done | bytes 786464 | tf_op jit(solution)/shard_map/ppermute | solution.py:18
  78.3 8.0 %attention.3 = bf16[384,512]{1,0:T(8,128)(2,1)S(1)} custom-call(s32[3,4]{1,0:T(4,128)S(1)} %add_select_fusion.offs, bf16[384,512]{1,0:T(8,128)(2,1)S(1)} %convolution_convert_fusion.4.q_ref, bf16[2,384,512]{2,1,0:T(8,128)(2,1)S(1)} %fusion.52.near_ref, bf16[2,384,512]{2,1,0:T(8,128)(2,1)S(1)} %fusion.55.rest_0_, ...), custom_call_target="tpu_custom_call" | custom-call | flops 1409286144 | bytes 4718592 | tf_op jit(solution)/shard_map/attention/pallas_call | solution.py:76
  86.3 1.6 %collective-permute-start.15 = (bf16[384,512]{1,0:T(8,128)(2,1)S(1)}, bf16[384,512]{1,0:T(8,128)(2,1)S(1)}, u32[]{:S(2)}, u32[]{:S(2)}) collective-permute-start(bf16[384,512]{1,0:T(8,128)(2,1)S(1)} %attention.3), channel_id=1, source_target_pairs={{0,1},{1,0},{2,3},{3,2},{4,5},{5,4},{6,7},{7,6},{8,9},{9,8},{10,11... | collective-permute-start | bytes 1179656 | tf_op jit(solution)/shard_map/ppermute | solution.py:18
  87.9 1.7 %broadcast_select_fusion.1 = (bf16[512,1024]{1,0:T(8,128)(2,1)S(1)}, bf16[512,1024]{1,0:T(8,128)(2,1)S(1)}) fusion(bf16[512,1024]{1,0:T(8,128)(2,1)} %param.11, bf16[512,1024]{1,0:T(8,128)(2,1)} %collective-permute-done.7, pred[]{:T(512)S(6)} %eq.5), kind=kLoop, calls=%fused_computation.78 | loop fusion | flops 1048576 | bytes 4194305 | tf_op jit(solution)/shard_map/jit(_where)/select_n | solution.py:141
  89.6 1.7 %collective-permute-done.3.rest_1_ = bf16[2,384,512]{2,1,0:T(8,128)(2,1)S(1)} collective-permute-done((bf16[2,384,512]{2,1,0:T(8,128)(2,1)S(1)}, bf16[2,384,512]{2,1,0:T(8,128)(2,1)S(1)}, u32[]{:S(2)}, u32[]{:S(2)}) %collective-permute-start.3) | collective-permute-done | bytes 786464 | tf_op jit(solution)/shard_map/ppermute | solution.py:18
  91.3 7.8 %attention.2 = bf16[384,512]{1,0:T(8,128)(2,1)S(1)} custom-call(s32[3,4]{1,0:T(4,128)S(1)} %add_select_fusion.offs, bf16[384,512]{1,0:T(8,128)(2,1)S(1)} %convolution_convert_fusion.5.q_ref, bf16[2,384,512]{2,1,0:T(8,128)(2,1)S(1)} %fusion.46.near_ref, bf16[2,384,512]{2,1,0:T(8,128)(2,1)S(1)} %fusion.49.rest_0_, ...), custom_call_target="tpu_custom_call" | custom-call | flops 1409286144 | bytes 4718592 | tf_op jit(solution)/shard_map/attention/pallas_call | solution.py:76
  99.1 1.6 %collective-permute-start.6 = (bf16[384,512]{1,0:T(8,128)(2,1)S(1)}, bf16[384,512]{1,0:T(8,128)(2,1)S(1)}, u32[]{:S(2)}, u32[]{:S(2)}) collective-permute-start(bf16[384,512]{1,0:T(8,128)(2,1)S(1)} %attention.2), channel_id=1, source_target_pairs={{0,1},{1,0},{2,3},{3,2},{4,5},{5,4},{6,7},{7,6},{8,9},{9,8},{10,11... | collective-permute-start | bytes 1179656 | tf_op jit(solution)/shard_map/ppermute | solution.py:18
  101.9 5.1 %collective-permute-done.6 = bf16[384,512]{1,0:T(8,128)(2,1)S(1)} collective-permute-done((bf16[384,512]{1,0:T(8,128)(2,1)S(1)}, bf16[384,512]{1,0:T(8,128)(2,1)S(1)}, u32[]{:S(2)}, u32[]{:S(2)}) %collective-permute-start.6) | collective-permute-done | bytes 393248 | tf_op jit(solution)/shard_map/ppermute | solution.py:18
  108.2 1.7 %fusion.7 = bf16[384,1536]{1,0:T(8,128)(2,1)S(1)} fusion(bf16[1024,1536]{1,0:T(8,128)(2,1)S(1)} %copy-done, bf16[384,1024]{1,0:T(8,128)(2,1)S(1)} %get-tuple-element.30, f32[384]{0:T(512)S(1)} %add_rsqrt_fusion.3), kind=kOutput, calls=%fused_computation.15 | convolution fusion | flops 1214447616 | bytes 5113344 | tf_op jit(solution)/shard_map/dot_general | solution.py:153
  113.4 1.7 %fusion.15 = bf16[384,1536]{1,0:T(8,128)(2,1)S(1)} fusion(bf16[1024,1536]{1,0:T(8,128)(2,1)S(1)} %copy-done, bf16[384,1024]{1,0:T(8,128)(2,1)S(1)} %get-tuple-element.28, f32[384]{0:T(512)S(1)} %add_rsqrt_fusion), kind=kOutput, calls=%fused_computation.23 | convolution fusion | flops 1214447616 | bytes 5113344 | tf_op jit(solution)/shard_map/dot_general | solution.py:153
  117.2 5.6 %collective-permute-done.8 = bf16[384,512]{1,0:T(8,128)(2,1)S(1)} collective-permute-done((bf16[384,512]{1,0:T(8,128)(2,1)}, bf16[384,512]{1,0:T(8,128)(2,1)S(1)}, u32[]{:S(2)}, u32[]{:S(2)}) %collective-permute-start.8) | collective-permute-done | bytes 393248 | tf_op jit(solution)/shard_map/ppermute | solution.py:18
  122.8 2.7 %fusion.94 = bf16[1,384,512]{2,1,0:T(8,128)(2,1)S(1)} fusion(bf16[384,512]{1,0:T(8,128)(2,1)S(1)} %collective-permute-done.8, bf16[384,1024]{1,0:T(8,128)(2,1)} %copy-done.11, pred[]{:T(512)S(6)} %eq.5, bf16[384,1536]{1,0:T(8,128)(2,1)} %copy-done.8, bf16[1536,1024]{1,0:T(8,128)(2,1)} %param.13, s32[]{:T(128)S(6)} %select_n.97), kind=kOutput, calls=%fused_computation.106 | convolution fusion | flops 605159424 | bytes 4325381 | tf_op jit(solution)/shard_map/dot_general | solution.py:157
  125.5 1.6 %collective-permute-done.16 = bf16[384,512]{1,0:T(8,128)(2,1)} collective-permute-done((bf16[384,512]{1,0:T(8,128)(2,1)}, bf16[384,512]{1,0:T(8,128)(2,1)}, u32[]{:S(2)}, u32[]{:S(2)}) %collective-permute-start.16) | collective-permute-done | bytes 393248 | tf_op jit(solution)/shard_map/ppermute | solution.py:18
  127.1 1.8 %fusion.95 = bf16[1,384,512]{2,1,0:T(8,128)(2,1)S(1)} fusion(bf16[384,512]{1,0:T(8,128)(2,1)} %collective-permute-done.16, bf16[384,1024]{1,0:T(8,128)(2,1)S(1)} %copy-done.10, pred[]{:T(512)S(6)} %eq.5, bf16[384,1536]{1,0:T(8,128)(2,1)S(1)} %copy-done.7, bf16[1536,1024]{1,0:T(8,128)(2,1)S(1)} %copy-done.4, s32[]{:T(128)S(6)} %select_n.97), kind=kOutput, calls=%fused_computation.107 | convolution fusion | flops 605159424 | bytes 4325381 | tf_op jit(solution)/shard_map/dot_general | solution.py:157
  (73 shorter events, 28.0 us)
Async XLA Ops:
  0.0 108.2 %copy-start = (bf16[1024,1536]{1,0:T(8,128)(2,1)S(1)}, bf16[1024,1536]{1,0:T(8,128)(2,1)}, u32[]{:S(2)}) copy-start(bf16[1024,1536]{1,0:T(8,128)(2,1)} %param.12) | copy-start | bytes 9437188
  0.0 10.2 %copy-start.5 = (s32[2]{0:T(128)S(1)}, s32[2]{0:T(128)}, u32[]{:S(2)}) copy-start(s32[2]{0:T(128)} %param.8) | copy-start | bytes 28
  0.0 10.3 %copy-start.1 = (s32[3,4]{1,0:T(4,128)S(1)}, s32[3,4]{1,0:T(4,128)}, u32[]{:S(2)}) copy-start(s32[3,4]{1,0:T(4,128)} %param.9) | copy-start | bytes 148
  2.2 31.2 %collective-permute-start.1 = (bf16[384,512]{1,0:T(8,128)(2,1)}, bf16[384,512]{1,0:T(8,128)(2,1)}, u32[]{:S(2)}, u32[]{:S(2)}) collective-permute-start(bf16[384,512]{1,0:T(8,128)(2,1)} %get-tuple-element.17), channel_id=1, source_target_pairs={{0,16},{2,18},{4,20},{6,22},{8,24},{10,26},{12,28},{14,30},{16,0},... | collective-permute-start | bytes 1179656 | tf_op jit(solution)/shard_map/ppermute | solution.py:18
  6.3 12.4 %collective-permute-start = (bf16[384,512]{1,0:T(8,128)(2,1)}, bf16[384,512]{1,0:T(8,128)(2,1)}, u32[]{:S(2)}, u32[]{:S(2)}) collective-permute-start(bf16[384,512]{1,0:T(8,128)(2,1)} %get-tuple-element.17), channel_id=1, source_target_pairs={{0,1},{1,0},{2,3},{3,2},{4,5},{5,4},{6,7},{7,6},{8,9},{9,8},{10,11... | collective-permute-start | bytes 1179656 | tf_op jit(solution)/shard_map/ppermute | solution.py:18
  7.8 33.1 %collective-permute-start.10 = (bf16[384,512]{1,0:T(8,128)(2,1)}, bf16[384,512]{1,0:T(8,128)(2,1)S(1)}, u32[]{:S(2)}, u32[]{:S(2)}) collective-permute-start(bf16[384,512]{1,0:T(8,128)(2,1)} %get-tuple-element.18), channel_id=1, source_target_pairs={{0,16},{2,18},{4,20},{6,22},{8,24},{10,26},{12,28},{14,30},{16,0},... | collective-permute-start | bytes 1179656 | tf_op jit(solution)/shard_map/ppermute | solution.py:18
  8.1 18.9 %collective-permute-start.9 = (bf16[384,512]{1,0:T(8,128)(2,1)}, bf16[384,512]{1,0:T(8,128)(2,1)}, u32[]{:S(2)}, u32[]{:S(2)}) collective-permute-start(bf16[384,512]{1,0:T(8,128)(2,1)} %get-tuple-element.18), channel_id=1, source_target_pairs={{0,1},{1,0},{2,3},{3,2},{4,5},{5,4},{6,7},{7,6},{8,9},{9,8},{10,11... | collective-permute-start | bytes 1179656 | tf_op jit(solution)/shard_map/ppermute | solution.py:18
  8.3 79.6 %collective-permute-start.7 = (bf16[512,1024]{1,0:T(8,128)(2,1)}, bf16[512,1024]{1,0:T(8,128)(2,1)}, u32[]{:S(2)}, u32[]{:S(2)}) collective-permute-start(bf16[512,1024]{1,0:T(8,128)(2,1)} %param.11), channel_id=1, source_target_pairs={{0,1},{1,0},{2,3},{3,2},{4,5},{5,4},{6,7},{7,6},{8,9},{9,8},{10,11... | collective-permute-start | bytes 3145736 | tf_op jit(solution)/shard_map/ppermute | solution.py:18
  10.4 18.4 %copy-start.2 = (bf16[3,1024,512]{2,1,0:T(8,128)(2,1)S(1)}, bf16[3,1024,512]{2,1,0:T(8,128)(2,1)}, u32[]{:S(2)}) copy-start(bf16[3,1024,512]{2,1,0:T(8,128)(2,1)} %param.10) | copy-start | bytes 9437188
  33.4 24.5 %collective-permute-start.2 = (bf16[384,512]{1,0:T(8,128)(2,1)}, bf16[384,512]{1,0:T(8,128)(2,1)S(1)}, u32[]{:S(2)}, u32[]{:S(2)}) collective-permute-start(bf16[384,512]{1,0:T(8,128)(2,1)} %collective-permute-done.1), channel_id=1, source_target_pairs={{0,1},{1,0},{2,3},{3,2},{4,5},{5,4},{6,7},{7,6},{8,9},{9,8},{10,11... | collective-permute-start | bytes 1179656 | tf_op jit(solution)/shard_map/ppermute | solution.py:18
  40.9 23.9 %collective-permute-start.11 = (bf16[384,512]{1,0:T(8,128)(2,1)S(1)}, bf16[384,512]{1,0:T(8,128)(2,1)S(1)}, u32[]{:S(2)}, u32[]{:S(2)}) collective-permute-start(bf16[384,512]{1,0:T(8,128)(2,1)S(1)} %collective-permute-done.10), channel_id=1, source_target_pairs={{0,1},{1,0},{2,3},{3,2},{4,5},{5,4},{6,7},{7,6},{8,9},{9,8},{10,11... | collective-permute-start | bytes 1179656 | tf_op jit(solution)/shard_map/ppermute | solution.py:18
  43.7 22.5 %collective-permute-start.14 = (bf16[2,384,512]{2,1,0:T(8,128)(2,1)S(1)}, bf16[2,384,512]{2,1,0:T(8,128)(2,1)S(1)}, u32[]{:S(2)}, u32[]{:S(2)}) collective-permute-start(bf16[2,384,512]{2,1,0:T(8,128)(2,1)S(1)} %fusion.52.near_ref), channel_id=1, source_target_pairs={{0,2},{2,0},{4,6},{6,4},{8,10},{10,8},{12,14},{14,12},{16,18},{18,... | collective-permute-start | bytes 2359304 | tf_op jit(solution)/shard_map/ppermute | solution.py:18
  43.8 24.0 %collective-permute-start.13 = (bf16[2,384,512]{2,1,0:T(8,128)(2,1)S(1)}, bf16[2,384,512]{2,1,0:T(8,128)(2,1)S(1)}, u32[]{:S(2)}, u32[]{:S(2)}) collective-permute-start(bf16[2,384,512]{2,1,0:T(8,128)(2,1)S(1)} %fusion.52.near_ref), channel_id=1, source_target_pairs={{0,4},{2,6},{4,0},{6,2},{8,12},{10,14},{12,8},{14,10},{16,20},{18,... | collective-permute-start | bytes 2359304 | tf_op jit(solution)/shard_map/ppermute | solution.py:18
  57.8 20.5 %collective-permute-start.12 = (bf16[2,384,512]{2,1,0:T(8,128)(2,1)S(1)}, bf16[2,384,512]{2,1,0:T(8,128)(2,1)S(1)}, u32[]{:S(2)}, u32[]{:S(2)}) collective-permute-start(bf16[2,384,512]{2,1,0:T(8,128)(2,1)S(1)} %fusion.52.near_ref), channel_id=1, source_target_pairs={{0,8},{2,10},{4,12},{6,14},{8,0},{10,2},{12,4},{14,6},{16,24},{18,... | collective-permute-start | bytes 2359304 | tf_op jit(solution)/shard_map/ppermute | solution.py:18
  64.8 24.8 %collective-permute-start.5 = (bf16[2,384,512]{2,1,0:T(8,128)(2,1)S(1)}, bf16[2,384,512]{2,1,0:T(8,128)(2,1)S(1)}, u32[]{:S(2)}, u32[]{:S(2)}) collective-permute-start(bf16[2,384,512]{2,1,0:T(8,128)(2,1)S(1)} %fusion.46.near_ref), channel_id=1, source_target_pairs={{0,2},{2,0},{4,6},{6,4},{8,10},{10,8},{12,14},{14,12},{16,18},{18,... | collective-permute-start | bytes 2359304 | tf_op jit(solution)/shard_map/ppermute | solution.py:18
  66.2 23.4 %collective-permute-start.4 = (bf16[2,384,512]{2,1,0:T(8,128)(2,1)S(1)}, bf16[2,384,512]{2,1,0:T(8,128)(2,1)S(1)}, u32[]{:S(2)}, u32[]{:S(2)}) collective-permute-start(bf16[2,384,512]{2,1,0:T(8,128)(2,1)S(1)} %fusion.46.near_ref), channel_id=1, source_target_pairs={{0,4},{2,6},{4,0},{6,2},{8,12},{10,14},{12,8},{14,10},{16,20},{18,... | collective-permute-start | bytes 2359304 | tf_op jit(solution)/shard_map/ppermute | solution.py:18
  67.8 23.5 %collective-permute-start.3 = (bf16[2,384,512]{2,1,0:T(8,128)(2,1)S(1)}, bf16[2,384,512]{2,1,0:T(8,128)(2,1)S(1)}, u32[]{:S(2)}, u32[]{:S(2)}) collective-permute-start(bf16[2,384,512]{2,1,0:T(8,128)(2,1)S(1)} %fusion.46.near_ref), channel_id=1, source_target_pairs={{0,8},{2,10},{4,12},{6,14},{8,0},{10,2},{12,4},{14,6},{16,24},{18,... | collective-permute-start | bytes 2359304 | tf_op jit(solution)/shard_map/ppermute | solution.py:18
  86.3 14.4 %collective-permute-start.15 = (bf16[384,512]{1,0:T(8,128)(2,1)S(1)}, bf16[384,512]{1,0:T(8,128)(2,1)S(1)}, u32[]{:S(2)}, u32[]{:S(2)}) collective-permute-start(bf16[384,512]{1,0:T(8,128)(2,1)S(1)} %attention.3), channel_id=1, source_target_pairs={{0,1},{1,0},{2,3},{3,2},{4,5},{5,4},{6,7},{7,6},{8,9},{9,8},{10,11... | collective-permute-start | bytes 1179656 | tf_op jit(solution)/shard_map/ppermute | solution.py:18
  99.1 7.8 %collective-permute-start.6 = (bf16[384,512]{1,0:T(8,128)(2,1)S(1)}, bf16[384,512]{1,0:T(8,128)(2,1)S(1)}, u32[]{:S(2)}, u32[]{:S(2)}) collective-permute-start(bf16[384,512]{1,0:T(8,128)(2,1)S(1)} %attention.2), channel_id=1, source_target_pairs={{0,1},{1,0},{2,3},{3,2},{4,5},{5,4},{6,7},{7,6},{8,9},{9,8},{10,11... | collective-permute-start | bytes 1179656 | tf_op jit(solution)/shard_map/ppermute | solution.py:18
  101.9 11.5 %copy-start.9 = (bf16[384,1024]{1,0:T(8,128)(2,1)}, bf16[384,1024]{1,0:T(8,128)(2,1)S(1)}, u32[]{:S(2)}) copy-start(bf16[384,1024]{1,0:T(8,128)(2,1)S(1)} %get-tuple-element.28) | copy-start | bytes 2359300
  111.9 10.9 %collective-permute-start.8 = (bf16[384,512]{1,0:T(8,128)(2,1)}, bf16[384,512]{1,0:T(8,128)(2,1)S(1)}, u32[]{:S(2)}, u32[]{:S(2)}) collective-permute-start(bf16[384,512]{1,0:T(8,128)(2,1)} %fusion.58), channel_id=1, source_target_pairs={{0,1},{1,0},{2,3},{3,2},{4,5},{5,4},{6,7},{7,6},{8,9},{9,8},{10,11... | collective-permute-start | bytes 1179656 | tf_op jit(solution)/shard_map/ppermute | solution.py:18
  116.7 10.4 %collective-permute-start.16 = (bf16[384,512]{1,0:T(8,128)(2,1)}, bf16[384,512]{1,0:T(8,128)(2,1)}, u32[]{:S(2)}, u32[]{:S(2)}) collective-permute-start(bf16[384,512]{1,0:T(8,128)(2,1)} %fusion.61), channel_id=1, source_target_pairs={{0,1},{1,0},{2,3},{3,2},{4,5},{5,4},{6,7},{7,6},{8,9},{9,8},{10,11... | collective-permute-start | bytes 1179656 | tf_op jit(solution)/shard_map/ppermute | solution.py:18
  117.2 9.9 %copy-start.7 = (bf16[384,1536]{1,0:T(8,128)(2,1)S(1)}, bf16[384,1536]{1,0:T(8,128)(2,1)}, u32[]{:S(2)}) copy-start(bf16[384,1536]{1,0:T(8,128)(2,1)} %copy-done.6) | copy-start | bytes 3538948
  117.2 9.9 %copy-start.10 = (bf16[384,1024]{1,0:T(8,128)(2,1)S(1)}, bf16[384,1024]{1,0:T(8,128)(2,1)}, u32[]{:S(2)}) copy-start(bf16[384,1024]{1,0:T(8,128)(2,1)} %copy-done.9) | copy-start | bytes 2359300
  (5 other events, 18.4 us)

commit v2 on v1

--- a/solution.py
+++ b/solution.py
@@ -11,17 +11,25 @@
 HEADS = 16
 BLOCK = 128
 LANES = 128
-RAW_SECTIONS = (0,)
 
 
 def partner(x, axis, bit):
     return lax.ppermute(x, axis, [(i, i ^ 1 << bit) for i in range(lax.axis_size(axis))])
 
 
-def both_halves(own, other, low):
-    first = jnp.where(low, own, other)
-    second = jnp.where(low, other, own)
-    return jnp.concatenate([first, second], axis=-1)
+def after(x, earlier):
+    return lax.optimization_barrier((x, earlier))[0]
+
+
+def join(own, other):
+    return jnp.concatenate([own, other], axis=-1)
+
+
+def halves_in_order(x, axis, keep):
+    first, second = jnp.split(x, 2, axis=axis)
+    return jnp.concatenate(
+        [jnp.where(keep, first, second), jnp.where(keep, second, first)], axis=axis
+    )
 
 
 def level_features(levels, model_width):
@@ -102,14 +110,16 @@
     low = me == 0
     bit_of = [axis_bits - 1 - s for s in range(sections)]
     offsets = (pairs % blocks_dev).astype(jnp.int32)
-    level_feat = level_features(levels, model_width)
+    level_feat = halves_in_order(level_features(levels, model_width), 1, low)
+    w_qkv, w_up, w_out_mine, w_out_sent = lax.optimization_barrier(
+        (
+            halves_in_order(w_qkv, 1, low),
+            halves_in_order(w_up, 0, low),
+            halves_in_order(w_out, 1, low),
+            halves_in_order(w_out, 1, jnp.logical_not(low)),
+        )
+    )
     w_q, w_kv = w_qkv[0], w_qkv[1:]
-
-    own = [noisy[s] for s in range(samples)]
-    other = [partner(x, "tp", 0) for x in own]
-    raw = [{c: partner(x, "seq", bit_of[c]) for c in RAW_SECTIONS} for x in own]
-    raw_other = [{c: partner(x, "tp", 0) for c, x in r.items()} for r in raw]
-    w_out_other = partner(w_out, "tp", 0)
 
     def condition(full, s):
         return (rms_norm(full.astype(jnp.float32)) + level_feat[s]).astype(jnp.bfloat16)
@@ -119,33 +129,41 @@
             "td,cde->cte", normed, w_kv, preferred_element_type=jnp.float32
         ).astype(jnp.bfloat16)
 
-    fulls, queries, nears, fars = [], [], [], []
+    own = [noisy[s] for s in range(samples)]
+    fulls, queries, nears, fars, arrived = [], [], [], [], []
+    other = raw = forwarded = None
     for s in range(samples):
-        full = both_halves(own[s], other[s], low)
+        mine_tp = own[s] if other is None else after(own[s], other)
+        mine_raw = own[s] if raw is None else after(own[s], raw)
+        other = partner(mine_tp, "tp", 0)
+        raw = partner(mine_raw, "seq", bit_of[0])
+        full = join(own[s], other)
         normed = condition(full, s)
         near = keys_values(normed)
-        far = {
-            c: partner(near, "seq", bit_of[c]) for c in range(sections) if c not in RAW_SECTIONS
-        }
+        far = {c: partner(near, "seq", bit_of[c]) for c in range(1, sections)}
+        forwarded = partner(raw, "tp", 0)
         query = jnp.dot(normed, w_q, preferred_element_type=jnp.float32).astype(jnp.bfloat16)
         fulls.append(full)
         nears.append(near)
         fars.append(far)
         queries.append(query)
-    for s in range(samples):
-        for c in RAW_SECTIONS:
-            far_full = both_halves(raw[s][c], raw_other[s][c], low)
-            fars[s][c] = keys_values(condition(far_full, s))
+        arrived.append((raw, forwarded))
+    first, second = jnp.split(after(w_out_sent, arrived[0][1]), 2, axis=0)
+    even = lax.axis_index("seq") % 2 == 0
+    fetched = partner(jnp.where(even, first, second), "tp", 0)
+    swapped = partner(fetched, "seq", 0)
+    w_out_other = [jnp.where(even, fetched, swapped), jnp.where(even, swapped, fetched)]
 
-    w_out_full = jnp.concatenate(
-        [jnp.where(low, w_out, w_out_other), jnp.where(low, w_out_other, w_out)], axis=0
-    )
+    w_out_full = jnp.concatenate([w_out_mine, *w_out_other], axis=0)
     w_mine = lax.dynamic_slice_in_dim(w_down, me * half_width, half_width, 1)
     w_theirs = lax.dynamic_slice_in_dim(w_down, (1 - me) * half_width, half_width, 1)
     outs = []
+    mixed = None
     for s in range(samples):
+        pair = arrived[s] if mixed is None else after(arrived[s], mixed)
+        fars[s][0] = keys_values(condition(join(*pair), s))
         mixed = attention(offsets, queries[s], nears[s], [fars[s][c] for c in range(sections)])
-        mixed_full = both_halves(mixed, partner(mixed, "tp", 0), low)
+        mixed_full = join(mixed, partner(mixed, "tp", 0))
         attn = jnp.dot(mixed_full, w_out_full, preferred_element_type=jnp.float32)
         middle = (fulls[s].astype(jnp.float32) + attn).astype(jnp.bfloat16)
         inner = rms_norm(middle.astype(jnp.float32)).astype(jnp.bfloat16)
@@ -155,7 +173,7 @@
         theirs = jnp.dot(hidden, w_theirs, preferred_element_type=jnp.float32)
         got = partner(theirs.astype(jnp.bfloat16), "tp", 0)
         mine = jnp.dot(hidden, w_mine, preferred_element_type=jnp.float32)
-        middle_half = jnp.where(low, middle[:, :half_width], middle[:, half_width:])
+        middle_half = middle[:, :half_width]
         outs.append(
             (middle_half.astype(jnp.float32) + mine + got.astype(jnp.float32)).astype(jnp.bfloat16)
         )

time: 130 us -> 115 us (0.88)
  waiting for transfers between devices: 63 us -> 32.2 us
  local copies, waits for them, and re-layouts: 2.66 us -> 13.2 us
  other arithmetic: 6.55 us -> 12.4 us
  starting transfers between devices: 22.9 us -> 18.4 us
  matrix products: 18.7 us -> 22.6 us
    ppermute x17 -> x18, waiting for transfers between devices: 63 us -> 32.2 us  [partner(): lax.ppermute(x, axis, [(i, i ^ 1 << bit) for i in range(lax.axis_size(axi...]
    unnamed x24 -> x34, local copies, waits for them, and re-layouts: 0.45 us -> 7.23 us
    concatenate x1 -> x4, other arithmetic: 0.01 us -> 5.57 us  [halves_in_order(): jnp.concatenate([jnp.where(keep, first, second), jnp.where(keep, second,...]
    ppermute x17 -> x18, starting transfers between devices: 22.9 us -> 18.4 us  [partner(): lax.ppermute(x, axis, [(i, i ^ 1 << bit) for i in range(lax.axis_size(axi...]
    split x0 -> x1, local copies, waits for them, and re-layouts: none -> 3.92 us  [halves_in_order(): first, second = jnp.split(x, 2, axis=axis)]
    dot_general x4, matrix products: 4.14 us -> 7.02 us  [keys_values(): jnp.einsum('td,cde->cte', normed, w_kv, preferred_element_type=jnp.float32)]
    reduce_sum x4, other arithmetic: 0.94 us -> 3.04 us  [rms_norm(): jnp.mean(values * values, axis=-1, keepdims=True) + 1e-06]
    select_n x6, other arithmetic: 4.45 us -> 2.8 us  [the longest x4 2.67 us: halves_in_order(): jnp.where(keep, first, second)]
  transfers between devices with their start and end apart: 17 -> 18, of which waited for: 11 -> 8; matrix products, arithmetic and copies ran while one was open for 14% -> 37% of each run, Pallas kernels for 12% -> 14%
where the time goes in v2:
time: 115 us
  waiting for transfers between devices  32.2 us (28%)
  matrix products  22.6 us (20%)
  starting transfers between devices  18.4 us (16%)
  Pallas kernels  15.9 us (14%)
  local copies, waits for them, and re-layouts  13.2 us (11%)
  other arithmetic  12.4 us (11%)
    ppermute x18, waiting for transfers between devices, partner(): lax.ppermute(x, axis, [(i, i ^ 1 << bit) for i in range(lax.axis_size(axi...  32.2 us
    ppermute x18, starting transfers between devices, partner(): lax.ppermute(x, axis, [(i, i ^ 1 << bit) for i in range(lax.axis_size(axi...  18.4 us
    pallas_call x2, Pallas kernels, attention(): pl.pallas_call(functools.partial(attention_kernel, sections, head_dim), o...  15.9 us
    unnamed x34, local copies, waits for them, and re-layouts  7.23 us
    dot_general x4, matrix products, keys_values(): jnp.einsum('td,cde->cte', normed, w_kv, preferred_element_type=jnp.float32)  7.02 us
    concatenate x4, other arithmetic, halves_in_order(): jnp.concatenate([jnp.where(keep, first, second), jnp.where(keep, second,...  5.57 us
    split x1, local copies, waits for them, and re-layouts, halves_in_order(): first, second = jnp.split(x, 2, axis=axis)  3.92 us
    dot_general x2, matrix products, per_device(): jnp.dot(inner, w_up, preferred_element_type=jnp.float32)  3.52 us
  transfers between devices with their start and end apart: 18, of which 8 were waited for; matrix products, arithmetic and copies ran while one was open for 37% of the time, Pallas kernels for 14%

profile of v2, /device:TPU:0, one launch (start us, length us, event | category | flops | bytes accessed | tf_op | source)
XLA Modules:
  0.0 115.1 jit_solution(11692232826233678435)
XLA Ops:
  0.0 2.1 %slice_bitcast_fusion = (bf16[384,512]{1,0:T(8,128)(2,1)S(1)}, bf16[384,512]{1,0:T(8,128)(2,1)}) fusion(bf16[2,384,512]{2,1,0:T(8,128)(2,1)} %param.7), kind=kLoop, calls=%fused_computation.117 | loop fusion | bytes 1572864 | tf_op jit(solution)/shard_map/squeeze | solution.py:132
  2.1 4.0 %collective-permute-start.1 = (bf16[384,512]{1,0:T(8,128)(2,1)}, bf16[384,512]{1,0:T(8,128)(2,1)}, u32[]{:S(2)}, u32[]{:S(2)}) collective-permute-start(bf16[384,512]{1,0:T(8,128)(2,1)} %get-tuple-element.36), channel_id=1, source_target_pairs={{0,16},{2,18},{4,20},{6,22},{8,24},{10,26},{12,28},{14,30},{16,0},... | collective-permute-start | bytes 1179656 | tf_op jit(solution)/shard_map/ppermute | solution.py:17
  7.6 3.9 %fusion.103 = (bf16[3,512,512]{2,1,0:T(8,128)(2,1)}, bf16[3,512,512]{2,1,0:T(8,128)(2,1)}) fusion(bf16[3,1024,512]{2,1,0:T(8,128)(2,1)} %param.10), kind=kLoop, calls=%fused_computation.143 | loop fusion | bytes 6291456 | tf_op jit(solution)/shard_map/split | solution.py:29
  11.6 2.6 %copy.18 = bf16[3,512,512]{1,2,0:T(8,128)(2,1)} copy(bf16[3,512,512]{2,1,0:T(8,128)(2,1)} %get-tuple-element.27) | data formatting | bytes 3145728
  14.2 2.6 %copy.19 = bf16[3,512,512]{1,2,0:T(8,128)(2,1)} copy(bf16[3,512,512]{2,1,0:T(8,128)(2,1)} %get-tuple-element.28) | data formatting | bytes 3145728
  16.8 2.2 %broadcast_select_fusion.1 = (bf16[512,1536]{1,0:T(8,128)(2,1)S(1)}, bf16[512,1536]{1,0:T(8,128)(2,1)S(1)}) fusion(pred[]{:T(512)S(6)} %eq.10, bf16[1024,1536]{1,0:T(8,128)(2,1)} %param.12), kind=kLoop, calls=%fused_computation.54 | loop fusion | flops 1572864 | bytes 6291457 | tf_op jit(solution)/shard_map/jit(_where)/select_n | solution.py:31
  21.1 1.8 %pad_maximum_fusion.1 = bf16[1024,1536]{1,0:T(8,128)(2,1)} fusion(bf16[512,1536]{1,0:T(8,128)(2,1)S(1)} %get-tuple-element.24, bf16[512,1536]{1,0:T(8,128)(2,1)S(1)} %get-tuple-element.23), kind=kLoop, calls=%fused_computation.3 | loop fusion | flops 6291456 | bytes 6291456 | tf_op jit(solution)/shard_map/concatenate | solution.py:30
  23.1 2.1 %pad_maximum_fusion = bf16[3,1024,512]{1,2,0:T(8,128)(2,1)} fusion(bf16[3,512,512]{1,2,0:T(8,128)(2,1)S(1)} %get-tuple-element.26, bf16[3,512,512]{1,2,0:T(8,128)(2,1)S(1)} %get-tuple-element.25), kind=kLoop, calls=%fused_computation.2 | loop fusion | flops 6291456 | bytes 6291456 | tf_op jit(solution)/shard_map/concatenate | solution.py:30
  25.1 1.7 %pad_maximum_fusion.3 = (bf16[512,1024]{1,0:T(8,128)(2,1)}, bf16[512,1024]{1,0:T(8,128)(2,1)}) fusion(bf16[512,512]{1,0:T(8,128)(2,1)S(1)} %get-tuple-element.33, bf16[512,512]{1,0:T(8,128)(2,1)S(1)} %get-tuple-element.32, bf16[512,512]{1,0:T(8,128)(2,1)S(1)} %get-tuple-element.34, bf16[512,512]{1,0:T(8,128)(2,1)S(1)} %get-tuple-element.31), kind=kLoop, calls=%fused_computation.77 | loop fusion | flops 4194304 | bytes 4194304 | tf_op jit(solution)/shard_map/concatenate | solution.py:30
  28.8 2.9 %fusion.42.near_ref = bf16[2,384,512]{2,1,0:T(8,128)(2,1)S(1)} fusion(bf16[3,1024,512]{1,2,0:T(8,128)(2,1)} %pad_maximum_fusion, f32[1024]{0:T(1024)S(1)} %bitcast.48, f32[384]{0:T(512)S(1)} %add_rsqrt_fusion.5, bf16[384,512]{1,0:T(8,128)(2,1)} %collective-permute-done, bf16[384,512]{1,0:T(8,128)(2,1)} %get-tuple-element.36), kind=kOutput, calls=%fused_computation.69 | convolution fusion | flops 808452096 | bytes 4724224 | tf_op jit(solution)/shard_map/td,cde->cte/dot_general | solution.py:128
  31.7 1.6 %collective-permute-start.3 = (bf16[2,384,512]{2,1,0:T(8,128)(2,1)S(1)}, bf16[2,384,512]{2,1,0:T(8,128)(2,1)S(1)}, u32[]{:S(2)}, u32[]{:S(2)}) collective-permute-start(bf16[2,384,512]{2,1,0:T(8,128)(2,1)S(1)} %fusion.42.near_ref), channel_id=1, source_target_pairs={{0,8},{2,10},{4,12},{6,14},{8,0},{10,2},{12,4},{14,6},{16,24},{18,... | collective-permute-start | bytes 2359304 | tf_op jit(solution)/shard_map/ppermute | solution.py:17
  36.3 1.7 %convolution_convert_fusion.5.q_ref = bf16[384,512]{1,0:T(8,128)(2,1)S(1)} fusion(bf16[3,1024,512]{1,2,0:T(8,128)(2,1)S(1)} %copy-done.5, f32[1024]{0:T(1024)S(1)} %bitcast.49, f32[384]{0:T(512)S(1)} %add_rsqrt_fusion.5, bf16[384,512]{1,0:T(8,128)(2,1)} %collective-permute-done, bf16[384,512]{1,0:T(8,128)(2,1)} %get-tuple-element.36), kind=kOutput, calls=%fused_computation.76 | convolution fusion | flops 405602304 | bytes 2234368 | tf_op jit(solution)/shard_map/dot_general | solution.py:145
  41.1 6.0 %collective-permute-done.10 = bf16[384,512]{1,0:T(8,128)(2,1)S(1)} collective-permute-done((bf16[384,512]{1,0:T(8,128)(2,1)S(1)}, bf16[384,512]{1,0:T(8,128)(2,1)S(1)}, u32[]{:S(2)}, u32[]{:S(2)}) %collective-permute-start.10) | collective-permute-done | bytes 393248 | tf_op jit(solution)/shard_map/ppermute | solution.py:17
  48.1 10.7 %collective-permute-done.11 = bf16[384,512]{1,0:T(8,128)(2,1)S(1)} collective-permute-done((bf16[384,512]{1,0:T(8,128)(2,1)S(1)}, bf16[384,512]{1,0:T(8,128)(2,1)S(1)}, u32[]{:S(2)}, u32[]{:S(2)}) %collective-permute-start.11) | collective-permute-done | bytes 393248 | tf_op jit(solution)/shard_map/ppermute | solution.py:17
  59.2 2.0 %fusion.43.rest_0_ = bf16[2,384,512]{2,1,0:T(8,128)(2,1)S(1)} fusion(bf16[3,1024,512]{1,2,0:T(8,128)(2,1)S(1)} %copy-done.5, f32[384]{0:T(512)S(1)} %add_rsqrt_fusion.4, f32[1024]{0:T(1024)S(1)} %bitcast.50, bf16[384,512]{1,0:T(8,128)(2,1)S(1)} %collective-permute-done.2, bf16[384,512]{1,0:T(8,128)(2,1)} %collective-permute-done.1), kind=kOutput, calls=%fused_computation.70 | convolution fusion | flops 808452096 | bytes 4724224 | tf_op jit(solution)/shard_map/td,cde->cte/dot_general | solution.py:128
  65.8 7.9 %attention.2 = bf16[384,512]{1,0:T(8,128)(2,1)S(1)} custom-call(s32[3,4]{1,0:T(4,128)S(1)} %add_select_fusion.offs, bf16[384,512]{1,0:T(8,128)(2,1)S(1)} %convolution_convert_fusion.5.q_ref, bf16[2,384,512]{2,1,0:T(8,128)(2,1)S(1)} %fusion.42.near_ref, bf16[2,384,512]{2,1,0:T(8,128)(2,1)S(1)} %fusion.43.rest_0_, ...), custom_call_target="tpu_custom_call" | custom-call | flops 1409286144 | bytes 4718592 | tf_op jit(solution)/shard_map/attention/pallas_call | solution.py:84
  75.8 3.8 %collective-permute-done.13.rest_1_ = bf16[2,384,512]{2,1,0:T(8,128)(2,1)S(1)} collective-permute-done((bf16[2,384,512]{2,1,0:T(8,128)(2,1)S(1)}, bf16[2,384,512]{2,1,0:T(8,128)(2,1)S(1)}, u32[]{:S(2)}, u32[]{:S(2)}) %collective-permute-start.13) | collective-permute-done | bytes 786464 | tf_op jit(solution)/shard_map/ppermute | solution.py:17
  80.6 8.1 %attention.3 = bf16[384,512]{1,0:T(8,128)(2,1)S(1)} custom-call(s32[3,4]{1,0:T(4,128)S(1)} %add_select_fusion.offs, bf16[384,512]{1,0:T(8,128)(2,1)S(1)} %convolution_convert_fusion.4.q_ref, bf16[2,384,512]{2,1,0:T(8,128)(2,1)S(1)} %fusion.44.near_ref, bf16[2,384,512]{2,1,0:T(8,128)(2,1)S(1)} %fusion.45.rest_0_, ...), custom_call_target="tpu_custom_call" | custom-call | flops 1409286144 | bytes 4718592 | tf_op jit(solution)/shard_map/attention/pallas_call | solution.py:84
  89.9 2.4 %fusion.19 = (f32[384]{0:T(512)S(1)}, bf16[384,1024]{1,0:T(8,128)(2,1)S(1)}) fusion(bf16[256,1024]{1,0:T(8,128)(2,1)S(1)} %get-tuple-element.30, bf16[256,1024]{1,0:T(8,128)(2,1)S(1)} %get-tuple-element.29, bf16[512,1024]{1,0:T(8,128)(2,1)S(1)} %copy-done.7, bf16[384,512]{1,0:T(8,128)(2,1)S(1)} %collective-permute-done.6, ...), kind=kOutput, calls=%fused_computation.38 | convolution fusion | flops 816709248 | bytes 4457984 | tf_op jit(solution)/shard_map/dot_general | solution.py:167
  92.3 1.8 %fusion.7 = bf16[384,1536]{1,0:T(8,128)(2,1)S(1)} fusion(bf16[1024,1536]{1,0:T(8,128)(2,1)S(1)} %copy-done.4, bf16[384,1024]{1,0:T(8,128)(2,1)S(1)} %get-tuple-element.44, f32[384]{0:T(512)S(1)} %add_rsqrt_fusion.3), kind=kOutput, calls=%fused_computation.17 | convolution fusion | flops 1214447616 | bytes 5113344 | tf_op jit(solution)/shard_map/dot_general | solution.py:171
  99.0 1.8 %fusion.15 = bf16[384,1536]{1,0:T(8,128)(2,1)S(1)} fusion(bf16[1024,1536]{1,0:T(8,128)(2,1)S(1)} %copy-done.4, bf16[384,1024]{1,0:T(8,128)(2,1)S(1)} %get-tuple-element.42, f32[384]{0:T(512)S(1)} %add_rsqrt_fusion), kind=kOutput, calls=%fused_computation.25 | convolution fusion | flops 1214447616 | bytes 5113344 | tf_op jit(solution)/shard_map/dot_general | solution.py:171
  103.1 4.9 %collective-permute-done.9 = bf16[384,512]{1,0:T(8,128)(2,1)} collective-permute-done((bf16[384,512]{1,0:T(8,128)(2,1)}, bf16[384,512]{1,0:T(8,128)(2,1)}, u32[]{:S(2)}, u32[]{:S(2)}) %collective-permute-start.9) | collective-permute-done | bytes 393248 | tf_op jit(solution)/shard_map/ppermute | solution.py:17
  108.0 2.3 %fusion.82 = bf16[1,384,512]{2,1,0:T(8,128)(2,1)S(1)} fusion(bf16[384,512]{1,0:T(8,128)(2,1)} %collective-permute-done.9, bf16[384,1024]{1,0:T(8,128)(2,1)} %copy-done.13, bf16[384,1536]{1,0:T(8,128)(2,1)} %copy-done.10, bf16[1536,1024]{1,0:T(8,128)(2,1)S(1)} %copy-done, s32[]{:T(128)S(6)} %select_n.114), kind=kOutput, calls=%fused_computation.115 | convolution fusion | flops 604962816 | bytes 3932164 | tf_op jit(solution)/shard_map/dot_general | solution.py:175
  110.3 3.1 %collective-permute-done.17 = bf16[384,512]{1,0:T(8,128)(2,1)S(1)} collective-permute-done((bf16[384,512]{1,0:T(8,128)(2,1)}, bf16[384,512]{1,0:T(8,128)(2,1)S(1)}, u32[]{:S(2)}, u32[]{:S(2)}) %collective-permute-start.17) | collective-permute-done | bytes 393248 | tf_op jit(solution)/shard_map/ppermute | solution.py:17
  (88 shorter events, 30.9 us)
Async XLA Ops:
  0.0 94.1 %copy-start = (bf16[1536,1024]{1,0:T(8,128)(2,1)S(1)}, bf16[1536,1024]{1,0:T(8,128)(2,1)}, u32[]{:S(2)}) copy-start(bf16[1536,1024]{1,0:T(8,128)(2,1)} %param.13) | copy-start | bytes 9437188
  2.1 26.1 %collective-permute-start.1 = (bf16[384,512]{1,0:T(8,128)(2,1)}, bf16[384,512]{1,0:T(8,128)(2,1)}, u32[]{:S(2)}, u32[]{:S(2)}) collective-permute-start(bf16[384,512]{1,0:T(8,128)(2,1)} %get-tuple-element.36), channel_id=1, source_target_pairs={{0,16},{2,18},{4,20},{6,22},{8,24},{10,26},{12,28},{14,30},{16,0},... | collective-permute-start | bytes 1179656 | tf_op jit(solution)/shard_map/ppermute | solution.py:17
  6.1 20.7 %collective-permute-start = (bf16[384,512]{1,0:T(8,128)(2,1)}, bf16[384,512]{1,0:T(8,128)(2,1)}, u32[]{:S(2)}, u32[]{:S(2)}) collective-permute-start(bf16[384,512]{1,0:T(8,128)(2,1)} %get-tuple-element.36), channel_id=1, source_target_pairs={{0,1},{1,0},{2,3},{3,2},{4,5},{5,4},{6,7},{7,6},{8,9},{9,8},{10,11... | collective-permute-start | bytes 1179656 | tf_op jit(solution)/shard_map/ppermute | solution.py:17
  28.2 11.3 %collective-permute-start.2 = (bf16[384,512]{1,0:T(8,128)(2,1)}, bf16[384,512]{1,0:T(8,128)(2,1)S(1)}, u32[]{:S(2)}, u32[]{:S(2)}) collective-permute-start(bf16[384,512]{1,0:T(8,128)(2,1)} %collective-permute-done.1), channel_id=1, source_target_pairs={{0,1},{1,0},{2,3},{3,2},{4,5},{5,4},{6,7},{7,6},{8,9},{9,8},{10,11... | collective-permute-start | bytes 1179656 | tf_op jit(solution)/shard_map/ppermute | solution.py:17
  28.8 7.6 %copy-start.5 = (bf16[3,1024,512]{1,2,0:T(8,128)(2,1)S(1)}, bf16[3,1024,512]{1,2,0:T(8,128)(2,1)}, u32[]{:S(2)}) copy-start(bf16[3,1024,512]{1,2,0:T(8,128)(2,1)} %pad_maximum_fusion) | copy-start | bytes 9437188
  31.7 30.6 %collective-permute-start.3 = (bf16[2,384,512]{2,1,0:T(8,128)(2,1)S(1)}, bf16[2,384,512]{2,1,0:T(8,128)(2,1)S(1)}, u32[]{:S(2)}, u32[]{:S(2)}) collective-permute-start(bf16[2,384,512]{2,1,0:T(8,128)(2,1)S(1)} %fusion.42.near_ref), channel_id=1, source_target_pairs={{0,8},{2,10},{4,12},{6,14},{8,0},{10,2},{12,4},{14,6},{16,24},{18,... | collective-permute-start | bytes 2359304 | tf_op jit(solution)/shard_map/ppermute | solution.py:17
  33.3 30.3 %collective-permute-start.4 = (bf16[2,384,512]{2,1,0:T(8,128)(2,1)S(1)}, bf16[2,384,512]{2,1,0:T(8,128)(2,1)S(1)}, u32[]{:S(2)}, u32[]{:S(2)}) collective-permute-start(bf16[2,384,512]{2,1,0:T(8,128)(2,1)S(1)} %fusion.42.near_ref), channel_id=1, source_target_pairs={{0,4},{2,6},{4,0},{6,2},{8,12},{10,14},{12,8},{14,10},{16,20},{18,... | collective-permute-start | bytes 2359304 | tf_op jit(solution)/shard_map/ppermute | solution.py:17
  34.8 30.3 %collective-permute-start.5 = (bf16[2,384,512]{2,1,0:T(8,128)(2,1)S(1)}, bf16[2,384,512]{2,1,0:T(8,128)(2,1)S(1)}, u32[]{:S(2)}, u32[]{:S(2)}) collective-permute-start(bf16[2,384,512]{2,1,0:T(8,128)(2,1)S(1)} %fusion.42.near_ref), channel_id=1, source_target_pairs={{0,2},{2,0},{4,6},{6,4},{8,10},{10,8},{12,14},{14,12},{16,18},{18,... | collective-permute-start | bytes 2359304 | tf_op jit(solution)/shard_map/ppermute | solution.py:17
  34.8 6.3 %copy-start.3 = (bf16[512,1024]{1,0:T(8,128)(2,1)S(1)}, bf16[512,1024]{1,0:T(8,128)(2,1)}, u32[]{:S(2)}) copy-start(bf16[512,1024]{1,0:T(8,128)(2,1)} %get-tuple-element.17) | copy-start | bytes 3145732
  34.8 12.4 %collective-permute-start.10 = (bf16[384,512]{1,0:T(8,128)(2,1)S(1)}, bf16[384,512]{1,0:T(8,128)(2,1)S(1)}, u32[]{:S(2)}, u32[]{:S(2)}) collective-permute-start(bf16[384,512]{1,0:T(8,128)(2,1)S(1)} %get-tuple-element.20), channel_id=1, source_target_pairs={{0,1},{1,0},{2,3},{3,2},{4,5},{5,4},{6,7},{7,6},{8,9},{9,8},{10,11... | collective-permute-start | bytes 1179656 | tf_op jit(solution)/shard_map/ppermute | solution.py:17
  39.5 19.3 %collective-permute-start.11 = (bf16[384,512]{1,0:T(8,128)(2,1)S(1)}, bf16[384,512]{1,0:T(8,128)(2,1)S(1)}, u32[]{:S(2)}, u32[]{:S(2)}) collective-permute-start(bf16[384,512]{1,0:T(8,128)(2,1)S(1)} %get-tuple-element.20), channel_id=1, source_target_pairs={{0,16},{2,18},{4,20},{6,22},{8,24},{10,26},{12,28},{14,30},{16,0},... | collective-permute-start | bytes 1179656 | tf_op jit(solution)/shard_map/ppermute | solution.py:17
  47.2 27.3 %collective-permute-start.7 = (bf16[256,1024]{1,0:T(8,128)(2,1)S(1)}, bf16[256,1024]{1,0:T(8,128)(2,1)S(1)}, u32[]{:S(2)}, u32[]{:S(2)}) collective-permute-start(bf16[256,1024]{1,0:T(8,128)(2,1)S(1)} %slice_select_fusion), channel_id=1, source_target_pairs={{0,1},{1,0},{2,3},{3,2},{4,5},{5,4},{6,7},{7,6},{8,9},{9,8},{10,11... | collective-permute-start | bytes 1572872 | tf_op jit(solution)/shard_map/ppermute | solution.py:17
  58.8 14.9 %collective-permute-start.12 = (bf16[384,512]{1,0:T(8,128)(2,1)S(1)}, bf16[384,512]{1,0:T(8,128)(2,1)S(1)}, u32[]{:S(2)}, u32[]{:S(2)}) collective-permute-start(bf16[384,512]{1,0:T(8,128)(2,1)S(1)} %collective-permute-done.11), channel_id=1, source_target_pairs={{0,1},{1,0},{2,3},{3,2},{4,5},{5,4},{6,7},{7,6},{8,9},{9,8},{10,11... | collective-permute-start | bytes 1179656 | tf_op jit(solution)/shard_map/ppermute | solution.py:17
  62.3 17.3 %collective-permute-start.13 = (bf16[2,384,512]{2,1,0:T(8,128)(2,1)S(1)}, bf16[2,384,512]{2,1,0:T(8,128)(2,1)S(1)}, u32[]{:S(2)}, u32[]{:S(2)}) collective-permute-start(bf16[2,384,512]{2,1,0:T(8,128)(2,1)S(1)} %fusion.44.near_ref), channel_id=1, source_target_pairs={{0,8},{2,10},{4,12},{6,14},{8,0},{10,2},{12,4},{14,6},{16,24},{18,... | collective-permute-start | bytes 2359304 | tf_op jit(solution)/shard_map/ppermute | solution.py:17
  63.6 17.0 %collective-permute-start.14 = (bf16[2,384,512]{2,1,0:T(8,128)(2,1)S(1)}, bf16[2,384,512]{2,1,0:T(8,128)(2,1)S(1)}, u32[]{:S(2)}, u32[]{:S(2)}) collective-permute-start(bf16[2,384,512]{2,1,0:T(8,128)(2,1)S(1)} %fusion.44.near_ref), channel_id=1, source_target_pairs={{0,4},{2,6},{4,0},{6,2},{8,12},{10,14},{12,8},{14,10},{16,20},{18,... | collective-permute-start | bytes 2359304 | tf_op jit(solution)/shard_map/ppermute | solution.py:17
  65.1 15.5 %collective-permute-start.15 = (bf16[2,384,512]{2,1,0:T(8,128)(2,1)S(1)}, bf16[2,384,512]{2,1,0:T(8,128)(2,1)S(1)}, u32[]{:S(2)}, u32[]{:S(2)}) collective-permute-start(bf16[2,384,512]{2,1,0:T(8,128)(2,1)S(1)} %fusion.44.near_ref), channel_id=1, source_target_pairs={{0,2},{2,0},{4,6},{6,4},{8,10},{10,8},{12,14},{14,12},{16,18},{18,... | collective-permute-start | bytes 2359304 | tf_op jit(solution)/shard_map/ppermute | solution.py:17
  73.7 15.9 %collective-permute-start.6 = (bf16[384,512]{1,0:T(8,128)(2,1)S(1)}, bf16[384,512]{1,0:T(8,128)(2,1)S(1)}, u32[]{:S(2)}, u32[]{:S(2)}) collective-permute-start(bf16[384,512]{1,0:T(8,128)(2,1)S(1)} %attention.2), channel_id=1, source_target_pairs={{0,1},{1,0},{2,3},{3,2},{4,5},{5,4},{6,7},{7,6},{8,9},{9,8},{10,11... | collective-permute-start | bytes 1179656 | tf_op jit(solution)/shard_map/ppermute | solution.py:17
  74.5 15.0 %collective-permute-start.8 = (bf16[256,1024]{1,0:T(8,128)(2,1)S(1)}, bf16[256,1024]{1,0:T(8,128)(2,1)S(1)}, u32[]{:S(2)}, u32[]{:S(2)}) collective-permute-start(bf16[256,1024]{1,0:T(8,128)(2,1)S(1)} %collective-permute-done.7), channel_id=1, source_target_pairs={{0,2},{2,0},{4,6},{6,4},{8,10},{10,8},{12,14},{14,12},{16,18},{18,... | collective-permute-start | bytes 1572872 | tf_op jit(solution)/shard_map/ppermute | solution.py:17
  88.7 9.2 %collective-permute-start.16 = (bf16[384,512]{1,0:T(8,128)(2,1)S(1)}, bf16[384,512]{1,0:T(8,128)(2,1)S(1)}, u32[]{:S(2)}, u32[]{:S(2)}) collective-permute-start(bf16[384,512]{1,0:T(8,128)(2,1)S(1)} %attention.3), channel_id=1, source_target_pairs={{0,1},{1,0},{2,3},{3,2},{4,5},{5,4},{6,7},{7,6},{8,9},{9,8},{10,11... | collective-permute-start | bytes 1179656 | tf_op jit(solution)/shard_map/ppermute | solution.py:17
  89.9 2.4 %copy-start.4 = (bf16[1024,1536]{1,0:T(8,128)(2,1)S(1)}, bf16[1024,1536]{1,0:T(8,128)(2,1)}, u32[]{:S(2)}) copy-start(bf16[1024,1536]{1,0:T(8,128)(2,1)} %pad_maximum_fusion.1) | copy-start | bytes 9437188
  95.6 12.4 %collective-permute-start.9 = (bf16[384,512]{1,0:T(8,128)(2,1)}, bf16[384,512]{1,0:T(8,128)(2,1)}, u32[]{:S(2)}, u32[]{:S(2)}) collective-permute-start(bf16[384,512]{1,0:T(8,128)(2,1)} %fusion.46), channel_id=1, source_target_pairs={{0,1},{1,0},{2,3},{3,2},{4,5},{5,4},{6,7},{7,6},{8,9},{9,8},{10,11... | collective-permute-start | bytes 1179656 | tf_op jit(solution)/shard_map/ppermute | solution.py:17
  102.4 11.0 %collective-permute-start.17 = (bf16[384,512]{1,0:T(8,128)(2,1)}, bf16[384,512]{1,0:T(8,128)(2,1)S(1)}, u32[]{:S(2)}, u32[]{:S(2)}) collective-permute-start(bf16[384,512]{1,0:T(8,128)(2,1)} %fusion.49), channel_id=1, source_target_pairs={{0,1},{1,0},{2,3},{3,2},{4,5},{5,4},{6,7},{7,6},{8,9},{9,8},{10,11... | collective-permute-start | bytes 1179656 | tf_op jit(solution)/shard_map/ppermute | solution.py:17
  103.1 10.3 %copy-start.12 = (bf16[384,1536]{1,0:T(8,128)(2,1)S(1)}, bf16[384,1536]{1,0:T(8,128)(2,1)}, u32[]{:S(2)}) copy-start(bf16[384,1536]{1,0:T(8,128)(2,1)} %copy-done.11) | copy-start | bytes 3538948
  103.1 10.3 %copy-start.15 = (bf16[384,1024]{1,0:T(8,128)(2,1)S(1)}, bf16[384,1024]{1,0:T(8,128)(2,1)}, u32[]{:S(2)}) copy-start(bf16[384,1024]{1,0:T(8,128)(2,1)} %copy-done.14) | copy-start | bytes 2359300
  (10 other events, 17.9 us)

commit v3 on v2

--- a/solution.py
+++ b/solution.py
@@ -25,23 +25,12 @@
     return jnp.concatenate([own, other], axis=-1)
 
 
-def halves_in_order(x, axis, keep):
-    first, second = jnp.split(x, 2, axis=axis)
-    return jnp.concatenate(
-        [jnp.where(keep, first, second), jnp.where(keep, second, first)], axis=axis
-    )
-
-
 def level_features(levels, model_width):
     half_count = model_width // 2
     index_row = jnp.arange(half_count, dtype=jnp.float32)
     freqs = jnp.exp(-math.log(10000.0) * index_row / half_count)
     angles = levels.astype(jnp.float32)[:, None] * freqs[None, :]
     return jnp.concatenate([jnp.sin(angles), jnp.cos(angles)], axis=1)
-
-
-def rms_norm(values):
-    return values * lax.rsqrt(jnp.mean(values * values, axis=-1, keepdims=True) + 1e-06)
 
 
 def attention_kernel(sections, head_dim, offs, q_ref, near_ref, *rest):
@@ -107,75 +96,87 @@
     blocks_dev = tok_rows // BLOCK
     axis_bits = lax.axis_size("seq").bit_length() - 1
     me = lax.axis_index("tp")
-    low = me == 0
     bit_of = [axis_bits - 1 - s for s in range(sections)]
     offsets = (pairs % blocks_dev).astype(jnp.int32)
-    level_feat = halves_in_order(level_features(levels, model_width), 1, low)
-    w_qkv, w_up, w_out_mine, w_out_sent = lax.optimization_barrier(
-        (
-            halves_in_order(w_qkv, 1, low),
-            halves_in_order(w_up, 0, low),
-            halves_in_order(w_out, 1, low),
-            halves_in_order(w_out, 1, jnp.logical_not(low)),
+    starts = (me * half_width, (1 - me) * half_width)
+    level_feat = level_features(levels, model_width)
+    level_halves = [lax.dynamic_slice_in_dim(level_feat, at, half_width, 1) for at in starts]
+    w_q = [lax.dynamic_slice_in_dim(w_qkv[0], at, half_width, 0) for at in starts]
+    w_kv = [lax.dynamic_slice_in_dim(w_qkv[1:], at, half_width, 1) for at in starts]
+    w_in = [lax.dynamic_slice_in_dim(w_up, at, half_width, 0) for at in starts]
+
+    def rms_halves(halves):
+        halves = [x.astype(jnp.float32) for x in halves]
+        squares = sum(jnp.sum(x * x, axis=-1, keepdims=True) for x in halves)
+        factor = lax.rsqrt(squares / model_width + 1e-06)
+        return [x * factor for x in halves]
+
+    def condition(halves, s):
+        return [
+            (x + feat[s]).astype(jnp.bfloat16) for x, feat in zip(rms_halves(halves), level_halves)
+        ]
+
+    def products(halves, weights):
+        return sum(
+            jnp.dot(x, w, preferred_element_type=jnp.float32) for x, w in zip(halves, weights)
         )
-    )
-    w_q, w_kv = w_qkv[0], w_qkv[1:]
-
-    def condition(full, s):
-        return (rms_norm(full.astype(jnp.float32)) + level_feat[s]).astype(jnp.bfloat16)
 
     def keys_values(normed):
-        return jnp.einsum(
-            "td,cde->cte", normed, w_kv, preferred_element_type=jnp.float32
+        return sum(
+            jnp.einsum("td,cde->cte", x, w, preferred_element_type=jnp.float32)
+            for x, w in zip(normed, w_kv)
         ).astype(jnp.bfloat16)
 
     own = [noisy[s] for s in range(samples)]
     fulls, queries, nears, fars, arrived = [], [], [], [], []
-    other = raw = forwarded = None
+    raw = None
     for s in range(samples):
-        mine_tp = own[s] if other is None else after(own[s], other)
         mine_raw = own[s] if raw is None else after(own[s], raw)
-        other = partner(mine_tp, "tp", 0)
+        other = partner(own[s], "tp", 0)
         raw = partner(mine_raw, "seq", bit_of[0])
-        full = join(own[s], other)
+        full = (own[s], other)
         normed = condition(full, s)
         near = keys_values(normed)
         far = {c: partner(near, "seq", bit_of[c]) for c in range(1, sections)}
         forwarded = partner(raw, "tp", 0)
-        query = jnp.dot(normed, w_q, preferred_element_type=jnp.float32).astype(jnp.bfloat16)
+        query = products(normed, w_q).astype(jnp.bfloat16)
         fulls.append(full)
         nears.append(near)
         fars.append(far)
         queries.append(query)
         arrived.append((raw, forwarded))
-    first, second = jnp.split(after(w_out_sent, arrived[0][1]), 2, axis=0)
+    first, second = jnp.split(after(w_out, arrived[0][1]), 2, axis=0)
     even = lax.axis_index("seq") % 2 == 0
     fetched = partner(jnp.where(even, first, second), "tp", 0)
     swapped = partner(fetched, "seq", 0)
     w_out_other = [jnp.where(even, fetched, swapped), jnp.where(even, swapped, fetched)]
 
-    w_out_full = jnp.concatenate([w_out_mine, *w_out_other], axis=0)
+    w_out_full = jnp.concatenate([w_out, *w_out_other], axis=0)
+    w_mixed = [lax.dynamic_slice_in_dim(w_out_full, at, half_width, 1) for at in starts]
     w_mine = lax.dynamic_slice_in_dim(w_down, me * half_width, half_width, 1)
     w_theirs = lax.dynamic_slice_in_dim(w_down, (1 - me) * half_width, half_width, 1)
     outs = []
     mixed = None
     for s in range(samples):
         pair = arrived[s] if mixed is None else after(arrived[s], mixed)
-        fars[s][0] = keys_values(condition(join(*pair), s))
+        fars[s][0] = keys_values(condition(pair, s))
         mixed = attention(offsets, queries[s], nears[s], [fars[s][c] for c in range(sections)])
-        mixed_full = join(mixed, partner(mixed, "tp", 0))
-        attn = jnp.dot(mixed_full, w_out_full, preferred_element_type=jnp.float32)
-        middle = (fulls[s].astype(jnp.float32) + attn).astype(jnp.bfloat16)
-        inner = rms_norm(middle.astype(jnp.float32)).astype(jnp.bfloat16)
-        hidden = jax.nn.gelu(
-            jnp.dot(inner, w_up, preferred_element_type=jnp.float32), approximate=True
-        ).astype(jnp.bfloat16)
+        received = partner(mixed, "tp", 0)
+        if s > 0:
+            received = after(received, theirs)
+        mixed_full = join(mixed, received)
+        middle = [
+            (x.astype(jnp.float32) + jnp.dot(mixed_full, w, preferred_element_type=jnp.float32))
+            .astype(jnp.bfloat16)
+            for x, w in zip(fulls[s], w_mixed)
+        ]
+        inner = [x.astype(jnp.bfloat16) for x in rms_halves(middle)]
+        hidden = jax.nn.gelu(products(inner, w_in), approximate=True).astype(jnp.bfloat16)
         theirs = jnp.dot(hidden, w_theirs, preferred_element_type=jnp.float32)
         got = partner(theirs.astype(jnp.bfloat16), "tp", 0)
         mine = jnp.dot(hidden, w_mine, preferred_element_type=jnp.float32)
-        middle_half = middle[:, :half_width]
         outs.append(
-            (middle_half.astype(jnp.float32) + mine + got.astype(jnp.float32)).astype(jnp.bfloat16)
+            (middle[0].astype(jnp.float32) + mine + got.astype(jnp.float32)).astype(jnp.bfloat16)
         )
     return jnp.stack(outs, axis=0)
 

time: 115 us -> 114 us (level)
  other arithmetic: 12.4 us -> 7.28 us
  starting transfers between devices: 18.4 us -> 23.5 us
  local copies, waits for them, and re-layouts: 13.2 us -> 8.8 us
  waiting for transfers between devices: 32.2 us -> 35.1 us
    unnamed x34 -> x12, local copies, waits for them, and re-layouts: 7.23 us -> 1.25 us
    slice x0 -> x3, local copies, waits for them, and re-layouts: none -> 5.36 us  [the longest x1 3.08 us: per_device(): w_qkv[1:]]
    concatenate x4 -> x2, other arithmetic: 5.57 us -> 0.21 us  [the longest x1 0.17 us: per_device(): w_out_full = jnp.concatenate([w_out, *w_out_other], axis=0)]
    ppermute x18, starting transfers between devices: 18.4 us -> 23.5 us  [partner(): lax.ppermute(x, axis, [(i, i ^ 1 << bit) for i in range(lax.axis_size(axi...]
    split x1 -> x0, local copies, waits for them, and re-layouts: 3.92 us -> none  [halves_in_order(): first, second = jnp.split(x, 2, axis=axis)]
    ppermute x18, waiting for transfers between devices: 32.2 us -> 35.1 us  [partner(): lax.ppermute(x, axis, [(i, i ^ 1 << bit) for i in range(lax.axis_size(axi...]
    select_n x4 -> x0, other arithmetic: 2.67 us -> none  [halves_in_order(): jnp.where(keep, first, second)]
    dot_general x10 -> x20, matrix products: 16.4 us -> 19 us  [the longest x8 8.5 us: keys_values(): jnp.einsum('td,cde->cte', x, w, preferred_element_type=jnp.float32)]
  transfers between devices with their start and end apart: 18 -> 18, of which waited for: 8 -> 6; matrix products, arithmetic and copies ran while one was open for 37% -> 29% of each run, Pallas kernels for 14% -> 14%
where the time goes in v3:
time: 114 us; the launch traced here: 113 us
  waiting for transfers between devices  35.1 us (31%)
  starting transfers between devices  23.5 us (21%)
  matrix products  22.2 us (19%)
  Pallas kernels  15.9 us (14%)
  local copies, waits for them, and re-layouts  8.8 us (8%)
  other arithmetic  7.28 us (6%)
    ppermute x18, waiting for transfers between devices, partner(): lax.ppermute(x, axis, [(i, i ^ 1 << bit) for i in range(lax.axis_size(axi...  35.1 us
    ppermute x18, starting transfers between devices, partner(): lax.ppermute(x, axis, [(i, i ^ 1 << bit) for i in range(lax.axis_size(axi...  23.5 us
    pallas_call x2, Pallas kernels, attention(): pl.pallas_call(functools.partial(attention_kernel, sections, head_dim), o...  15.9 us
    dot_general x8, matrix products, keys_values(): jnp.einsum('td,cde->cte', x, w, preferred_element_type=jnp.float32)  8.5 us
    dot_general x8, matrix products, products(): jnp.dot(x, w, preferred_element_type=jnp.float32)  6.82 us
    reduce_sum x7, other arithmetic, rms_halves(): squares = sum((jnp.sum(x * x, axis=-1, keepdims=True) for x in halves))  4.43 us
    dot_general x4, matrix products, per_device(): jnp.dot(mixed_full, w, preferred_element_type=jnp.float32)  3.64 us
    slice x1, local copies, waits for them, and re-layouts, per_device(): w_qkv[1:]  3.08 us
  transfers between devices with their start and end apart: 18, of which 6 were waited for; matrix products, arithmetic and copies ran while one was open for 29% of the time, Pallas kernels for 14%

profile of v3, /device:TPU:0, one launch (start us, length us, event | category | flops | bytes accessed | tf_op | source)
XLA Modules:
  0.0 113.1 jit_solution(181851385474620460)
XLA Ops:
  0.0 2.2 %slice_bitcast_fusion = (bf16[384,512]{1,0:T(8,128)(2,1)}, bf16[384,512]{1,0:T(8,128)(2,1)}) fusion(bf16[2,384,512]{2,1,0:T(8,128)(2,1)} %param.7), kind=kLoop, calls=%fused_computation.179 | loop fusion | bytes 1572864 | tf_op jit(solution)/shard_map/squeeze | solution.py:130
  2.2 3.0 %collective-permute-start = (bf16[384,512]{1,0:T(8,128)(2,1)}, bf16[384,512]{1,0:T(8,128)(2,1)}, u32[]{:S(2)}, u32[]{:S(2)}) collective-permute-start(bf16[384,512]{1,0:T(8,128)(2,1)} %get-tuple-element.20), channel_id=1, source_target_pairs={{0,1},{1,0},{2,3},{3,2},{4,5},{5,4},{6,7},{7,6},{8,9},{9,8},{10,11... | collective-permute-start | bytes 1179656 | tf_op jit(solution)/shard_map/ppermute | solution.py:17
  5.2 2.6 %collective-permute-start.1 = (bf16[384,512]{1,0:T(8,128)(2,1)}, bf16[384,512]{1,0:T(8,128)(2,1)}, u32[]{:S(2)}, u32[]{:S(2)}) collective-permute-start(bf16[384,512]{1,0:T(8,128)(2,1)} %get-tuple-element.20), channel_id=1, source_target_pairs={{0,16},{2,18},{4,20},{6,22},{8,24},{10,26},{12,28},{14,30},{16,0},... | collective-permute-start | bytes 1179656 | tf_op jit(solution)/shard_map/ppermute | solution.py:17
  9.8 2.3 %slice.32 = bf16[1,1024,512]{2,1,0:T(8,128)(2,1)} slice(bf16[3,1024,512]{2,1,0:T(8,128)(2,1)} %param.10), slice={[0:1], [0:1024], [0:512]} | slice | bytes 2097152 | tf_op jit(solution)/shard_map/slice | solution.py:104
  12.1 3.1 %slice.34 = bf16[2,1024,512]{2,1,0:T(8,128)(2,1)} slice(bf16[3,1024,512]{2,1,0:T(8,128)(2,1)} %param.10), slice={[1:3], [0:1024], [0:512]} | slice | bytes 4194304 | tf_op jit(solution)/shard_map/slice | solution.py:105
  17.9 2.0 %fusion.91 = f32[2,512,384]{1,2,0:T(8,128)S(1)} fusion(bf16[2,1024,512]{2,1,0:T(8,128)(2,1)} %slice.34, s32[]{:T(128)S(6)} %select_n.46, f32[512]{0:T(512)S(1)} %bitcast.87, f32[384]{0:T(512)S(1)} %add_rsqrt_fusion.5, bf16[2,384,512]{2,1,0:T(8,128)(2,1)} %param.7), kind=kOutput, calls=%fused_computation.131 | convolution fusion | flops 403439616 | bytes 3018244 | tf_op jit(solution)/shard_map/td,cde->cte/dot_general | solution.py:126
  19.9 1.8 %fusion.30.near_ref = bf16[2,384,512]{2,1,0:T(8,128)(2,1)S(1)} fusion(f32[2,512,384]{1,2,0:T(8,128)S(1)} %fusion.91, bf16[2,1024,512]{2,1,0:T(8,128)(2,1)S(1)} %copy-done.1, s32[]{:T(128)S(6)} %select_n.47, bf16[384,512]{1,0:T(8,128)(2,1)} %collective-permute-done, f32[512]{0:T(512)S(1)} %bitcast.84, f32[384]{0:T(512)S(1)} %add_rsqrt_fusion.5), kind=kOutput, calls=%fused_computation.39 | convolution fusion | flops 404226048 | bytes 3805188 | tf_op jit(solution)/shard_map/td,cde->cte/dot_general | solution.py:126
  21.7 1.6 %collective-permute-start.4 = (bf16[2,384,512]{2,1,0:T(8,128)(2,1)S(1)}, bf16[2,384,512]{2,1,0:T(8,128)(2,1)S(1)}, u32[]{:S(2)}, u32[]{:S(2)}) collective-permute-start(bf16[2,384,512]{2,1,0:T(8,128)(2,1)S(1)} %fusion.30.near_ref), channel_id=1, source_target_pairs={{0,4},{2,6},{4,0},{6,2},{8,12},{10,14},{12,8},{14,10},{16,20},{18,... | collective-permute-start | bytes 2359304 | tf_op jit(solution)/shard_map/ppermute | solution.py:17
  23.3 1.6 %collective-permute-start.3 = (bf16[2,384,512]{2,1,0:T(8,128)(2,1)S(1)}, bf16[2,384,512]{2,1,0:T(8,128)(2,1)S(1)}, u32[]{:S(2)}, u32[]{:S(2)}) collective-permute-start(bf16[2,384,512]{2,1,0:T(8,128)(2,1)S(1)} %fusion.30.near_ref), channel_id=1, source_target_pairs={{0,8},{2,10},{4,12},{6,14},{8,0},{10,2},{12,4},{14,6},{16,24},{18,... | collective-permute-start | bytes 2359304 | tf_op jit(solution)/shard_map/ppermute | solution.py:17
  26.6 1.9 %collective-permute-start.11 = (bf16[384,512]{1,0:T(8,128)(2,1)}, bf16[384,512]{1,0:T(8,128)(2,1)S(1)}, u32[]{:S(2)}, u32[]{:S(2)}) collective-permute-start(bf16[384,512]{1,0:T(8,128)(2,1)} %get-tuple-element.11), channel_id=1, source_target_pairs={{0,16},{2,18},{4,20},{6,22},{8,24},{10,26},{12,28},{14,30},{16,0},... | collective-permute-start | bytes 1179656 | tf_op jit(solution)/shard_map/ppermute | solution.py:17
  33.7 5.6 %collective-permute-done.2 = bf16[384,512]{1,0:T(8,128)(2,1)S(1)} collective-permute-done((bf16[384,512]{1,0:T(8,128)(2,1)}, bf16[384,512]{1,0:T(8,128)(2,1)S(1)}, u32[]{:S(2)}, u32[]{:S(2)}) %collective-permute-start.2) | collective-permute-done | bytes 393248 | tf_op jit(solution)/shard_map/ppermute | solution.py:17
  39.5 11.0 %collective-permute-done.11 = bf16[384,512]{1,0:T(8,128)(2,1)S(1)} collective-permute-done((bf16[384,512]{1,0:T(8,128)(2,1)}, bf16[384,512]{1,0:T(8,128)(2,1)S(1)}, u32[]{:S(2)}, u32[]{:S(2)}) %collective-permute-start.11) | collective-permute-done | bytes 393248 | tf_op jit(solution)/shard_map/ppermute | solution.py:17
  52.0 1.6 %fusion.85 = f32[2,512,384]{1,2,0:T(8,128)S(1)} fusion(bf16[2,1024,512]{2,1,0:T(8,128)(2,1)S(1)} %copy-done.1, s32[]{:T(128)S(6)} %select_n.46, bf16[384,512]{1,0:T(8,128)(2,1)} %collective-permute-done.1, f32[384]{0:T(512)S(1)} %add_rsqrt_fusion.4, f32[512]{0:T(512)S(1)} %bitcast.89), kind=kOutput, calls=%fused_computation.125 | convolution fusion | flops 403439616 | bytes 3018756 | tf_op jit(solution)/shard_map/td,cde->cte/dot_general | solution.py:126
  55.6 2.7 %collective-permute-start.13 = (bf16[2,384,512]{2,1,0:T(8,128)(2,1)S(1)}, bf16[2,384,512]{2,1,0:T(8,128)(2,1)S(1)}, u32[]{:S(2)}, u32[]{:S(2)}) collective-permute-start(bf16[2,384,512]{2,1,0:T(8,128)(2,1)S(1)} %fusion.32.near_ref), channel_id=1, source_target_pairs={{0,8},{2,10},{4,12},{6,14},{8,0},{10,2},{12,4},{14,6},{16,24},{18,... | collective-permute-start | bytes 2359304 | tf_op jit(solution)/shard_map/ppermute | solution.py:17
  58.7 7.9 %attention.2 = bf16[384,512]{1,0:T(8,128)(2,1)S(1)} custom-call(s32[3,4]{1,0:T(4,128)S(1)} %add_select_fusion.offs, bf16[384,512]{1,0:T(8,128)(2,1)S(1)} %fusion.40.q_ref, bf16[2,384,512]{2,1,0:T(8,128)(2,1)S(1)} %fusion.30.near_ref, bf16[2,384,512]{2,1,0:T(8,128)(2,1)S(1)} %fusion.31.rest_0_, bf16[2,384,512]{2,1,0:T(8,128)(2,1)S(1)} %collective-permute-done.3.rest_1_, ...), custom_call_target="tpu_custom_call" | custom-call | flops 1409286144 | bytes 4718592 | tf_op jit(solution)/shard_map/attention/pallas_call | solution.py:73
  66.6 1.6 %collective-permute-start.6 = (bf16[384,512]{1,0:T(8,128)(2,1)S(1)}, bf16[384,512]{1,0:T(8,128)(2,1)S(1)}, u32[]{:S(2)}, u32[]{:S(2)}) collective-permute-start(bf16[384,512]{1,0:T(8,128)(2,1)S(1)} %attention.2), channel_id=1, source_target_pairs={{0,1},{1,0},{2,3},{3,2},{4,5},{5,4},{6,7},{7,6},{8,9},{9,8},{10,11... | collective-permute-start | bytes 1179656 | tf_op jit(solution)/shard_map/ppermute | solution.py:17
  68.5 5.1 %collective-permute-done.7 = bf16[256,1024]{1,0:T(8,128)(2,1)S(1)} collective-permute-done((bf16[256,1024]{1,0:T(8,128)(2,1)S(1)}, bf16[256,1024]{1,0:T(8,128)(2,1)S(1)}, u32[]{:S(2)}, u32[]{:S(2)}) %collective-permute-start.7) | collective-permute-done | bytes 524320 | tf_op jit(solution)/shard_map/ppermute | solution.py:17
  74.9 8.1 %attention.3 = bf16[384,512]{1,0:T(8,128)(2,1)S(1)} custom-call(s32[3,4]{1,0:T(4,128)S(1)} %add_select_fusion.offs, bf16[384,512]{1,0:T(8,128)(2,1)S(1)} %fusion.41.q_ref, bf16[2,384,512]{2,1,0:T(8,128)(2,1)S(1)} %fusion.32.near_ref, bf16[2,384,512]{2,1,0:T(8,128)(2,1)S(1)} %fusion.33.rest_0_, bf16[2,384,512]{2,1,0:T(8,128)(2,1)S(1)} %collective-permute-done.13.rest_1_, ...), custom_call_target="tpu_custom_call" | custom-call | flops 1409286144 | bytes 4718592 | tf_op jit(solution)/shard_map/attention/pallas_call | solution.py:73
  83.0 1.8 %collective-permute-start.16 = (bf16[384,512]{1,0:T(8,128)(2,1)S(1)}, bf16[384,512]{1,0:T(8,128)(2,1)S(1)}, u32[]{:S(2)}, u32[]{:S(2)}) collective-permute-start(bf16[384,512]{1,0:T(8,128)(2,1)S(1)} %attention.3), channel_id=1, source_target_pairs={{0,1},{1,0},{2,3},{3,2},{4,5},{5,4},{6,7},{7,6},{8,9},{9,8},{10,11... | collective-permute-start | bytes 1179656 | tf_op jit(solution)/shard_map/ppermute | solution.py:17
  85.0 1.7 %multiply_reduce_fusion.2 = (f32[384]{0:T(512)S(1)}, f32[384,512]{1,0:T(8,128)S(1)}) fusion(bf16[1024,1024]{1,0:T(8,128)(2,1)S(1)} %pad_maximum_fusion, s32[]{:T(128)S(6)} %select_n.47, bf16[384,512]{1,0:T(8,128)(2,1)S(1)} %collective-permute-done.6, bf16[384,512]{1,0:T(8,128)(2,1)S(1)} %attention.2, bf16[384,512]{1,0:T(8,128)(2,1)} %collective-permute-done), kind=kOutput, calls=%fused_computation.118 | convolution fusion | flops 405405312 | bytes 3016196 | tf_op jit(solution)/shard_map/dot_general | solution.py:169
  91.3 3.7 %collective-permute-done.16 = bf16[384,512]{1,0:T(8,128)(2,1)S(1)} collective-permute-done((bf16[384,512]{1,0:T(8,128)(2,1)S(1)}, bf16[384,512]{1,0:T(8,128)(2,1)S(1)}, u32[]{:S(2)}, u32[]{:S(2)}) %collective-permute-start.16) | collective-permute-done | bytes 393248 | tf_op jit(solution)/shard_map/ppermute | solution.py:17
  99.1 1.8 %collective-permute-start.17 = (bf16[384,512]{1,0:T(8,128)(2,1)S(1)}, bf16[384,512]{1,0:T(8,128)(2,1)S(1)}, u32[]{:S(2)}, u32[]{:S(2)}) collective-permute-start(bf16[384,512]{1,0:T(8,128)(2,1)S(1)} %fusion.50), channel_id=1, source_target_pairs={{0,1},{1,0},{2,3},{3,2},{4,5},{5,4},{6,7},{7,6},{8,9},{9,8},{10,11... | collective-permute-start | bytes 1179656 | tf_op jit(solution)/shard_map/ppermute | solution.py:17
  100.9 2.5 %collective-permute-done.9 = bf16[384,512]{1,0:T(8,128)(2,1)S(1)} collective-permute-done((bf16[384,512]{1,0:T(8,128)(2,1)S(1)}, bf16[384,512]{1,0:T(8,128)(2,1)S(1)}, u32[]{:S(2)}, u32[]{:S(2)}) %collective-permute-start.9) | collective-permute-done | bytes 393248 | tf_op jit(solution)/shard_map/ppermute | solution.py:17
  104.2 7.2 %collective-permute-done.17 = bf16[384,512]{1,0:T(8,128)(2,1)S(1)} collective-permute-done((bf16[384,512]{1,0:T(8,128)(2,1)S(1)}, bf16[384,512]{1,0:T(8,128)(2,1)S(1)}, u32[]{:S(2)}, u32[]{:S(2)}) %collective-permute-start.17) | collective-permute-done | bytes 393248 | tf_op jit(solution)/shard_map/ppermute | solution.py:17
  (76 shorter events, 28.8 us)
Async XLA Ops:
  0.0 87.4 %copy-start = (bf16[1024,1536]{1,0:T(8,128)(2,1)S(1)}, bf16[1024,1536]{1,0:T(8,128)(2,1)}, u32[]{:S(2)}) copy-start(bf16[1024,1536]{1,0:T(8,128)(2,1)} %param.12) | copy-start | bytes 9437188
  2.2 14.5 %collective-permute-start = (bf16[384,512]{1,0:T(8,128)(2,1)}, bf16[384,512]{1,0:T(8,128)(2,1)}, u32[]{:S(2)}, u32[]{:S(2)}) collective-permute-start(bf16[384,512]{1,0:T(8,128)(2,1)} %get-tuple-element.20), channel_id=1, source_target_pairs={{0,1},{1,0},{2,3},{3,2},{4,5},{5,4},{6,7},{7,6},{8,9},{9,8},{10,11... | collective-permute-start | bytes 1179656 | tf_op jit(solution)/shard_map/ppermute | solution.py:17
  5.2 21.4 %collective-permute-start.1 = (bf16[384,512]{1,0:T(8,128)(2,1)}, bf16[384,512]{1,0:T(8,128)(2,1)}, u32[]{:S(2)}, u32[]{:S(2)}) collective-permute-start(bf16[384,512]{1,0:T(8,128)(2,1)} %get-tuple-element.20), channel_id=1, source_target_pairs={{0,16},{2,18},{4,20},{6,22},{8,24},{10,26},{12,28},{14,30},{16,0},... | collective-permute-start | bytes 1179656 | tf_op jit(solution)/shard_map/ppermute | solution.py:17
  7.7 17.5 %collective-permute-start.10 = (bf16[384,512]{1,0:T(8,128)(2,1)}, bf16[384,512]{1,0:T(8,128)(2,1)S(1)}, u32[]{:S(2)}, u32[]{:S(2)}) collective-permute-start(bf16[384,512]{1,0:T(8,128)(2,1)} %get-tuple-element.11), channel_id=1, source_target_pairs={{0,1},{1,0},{2,3},{3,2},{4,5},{5,4},{6,7},{7,6},{8,9},{9,8},{10,11... | collective-permute-start | bytes 1179656 | tf_op jit(solution)/shard_map/ppermute | solution.py:17
  15.2 4.7 %copy-start.1 = (bf16[2,1024,512]{2,1,0:T(8,128)(2,1)S(1)}, bf16[2,1024,512]{2,1,0:T(8,128)(2,1)}, u32[]{:S(2)}) copy-start(bf16[2,1024,512]{2,1,0:T(8,128)(2,1)} %slice.34) | copy-start | bytes 6291460
  19.8 5.0 %copy-start.2 = (bf16[2,384,512]{2,1,0:T(8,128)(2,1)S(1)}, bf16[2,384,512]{2,1,0:T(8,128)(2,1)}, u32[]{:S(2)}) copy-start(bf16[2,384,512]{2,1,0:T(8,128)(2,1)} %param.7) | copy-start | bytes 2359300
  19.8 5.0 %copy-start.3 = (bf16[1,1024,512]{2,1,0:T(8,128)(2,1)S(1)}, bf16[1,1024,512]{2,1,0:T(8,128)(2,1)}, u32[]{:S(2)}) copy-start(bf16[1,1024,512]{2,1,0:T(8,128)(2,1)} %slice.32) | copy-start | bytes 3145732
  21.6 33.3 %collective-permute-start.5 = (bf16[2,384,512]{2,1,0:T(8,128)(2,1)S(1)}, bf16[2,384,512]{2,1,0:T(8,128)(2,1)S(1)}, u32[]{:S(2)}, u32[]{:S(2)}) collective-permute-start(bf16[2,384,512]{2,1,0:T(8,128)(2,1)S(1)} %fusion.30.near_ref), channel_id=1, source_target_pairs={{0,2},{2,0},{4,6},{6,4},{8,10},{10,8},{12,14},{14,12},{16,18},{18,... | collective-permute-start | bytes 2359304 | tf_op jit(solution)/shard_map/ppermute | solution.py:17
  21.7 33.8 %collective-permute-start.4 = (bf16[2,384,512]{2,1,0:T(8,128)(2,1)S(1)}, bf16[2,384,512]{2,1,0:T(8,128)(2,1)S(1)}, u32[]{:S(2)}, u32[]{:S(2)}) collective-permute-start(bf16[2,384,512]{2,1,0:T(8,128)(2,1)S(1)} %fusion.30.near_ref), channel_id=1, source_target_pairs={{0,4},{2,6},{4,0},{6,2},{8,12},{10,14},{12,8},{14,10},{16,20},{18,... | collective-permute-start | bytes 2359304 | tf_op jit(solution)/shard_map/ppermute | solution.py:17
  23.3 34.9 %collective-permute-start.3 = (bf16[2,384,512]{2,1,0:T(8,128)(2,1)S(1)}, bf16[2,384,512]{2,1,0:T(8,128)(2,1)S(1)}, u32[]{:S(2)}, u32[]{:S(2)}) collective-permute-start(bf16[2,384,512]{2,1,0:T(8,128)(2,1)S(1)} %fusion.30.near_ref), channel_id=1, source_target_pairs={{0,8},{2,10},{4,12},{6,14},{8,0},{10,2},{12,4},{14,6},{16,24},{18,... | collective-permute-start | bytes 2359304 | tf_op jit(solution)/shard_map/ppermute | solution.py:17
  26.6 24.0 %collective-permute-start.11 = (bf16[384,512]{1,0:T(8,128)(2,1)}, bf16[384,512]{1,0:T(8,128)(2,1)S(1)}, u32[]{:S(2)}, u32[]{:S(2)}) collective-permute-start(bf16[384,512]{1,0:T(8,128)(2,1)} %get-tuple-element.11), channel_id=1, source_target_pairs={{0,16},{2,18},{4,20},{6,22},{8,24},{10,26},{12,28},{14,30},{16,0},... | collective-permute-start | bytes 1179656 | tf_op jit(solution)/shard_map/ppermute | solution.py:17
  28.5 10.8 %collective-permute-start.2 = (bf16[384,512]{1,0:T(8,128)(2,1)}, bf16[384,512]{1,0:T(8,128)(2,1)S(1)}, u32[]{:S(2)}, u32[]{:S(2)}) collective-permute-start(bf16[384,512]{1,0:T(8,128)(2,1)} %collective-permute-done.1), channel_id=1, source_target_pairs={{0,1},{1,0},{2,3},{3,2},{4,5},{5,4},{6,7},{7,6},{8,9},{9,8},{10,11... | collective-permute-start | bytes 1179656 | tf_op jit(solution)/shard_map/ppermute | solution.py:17
  39.3 35.6 %collective-permute-start.15 = (bf16[2,384,512]{2,1,0:T(8,128)(2,1)S(1)}, bf16[2,384,512]{2,1,0:T(8,128)(2,1)S(1)}, u32[]{:S(2)}, u32[]{:S(2)}) collective-permute-start(bf16[2,384,512]{2,1,0:T(8,128)(2,1)S(1)} %fusion.32.near_ref), channel_id=1, source_target_pairs={{0,2},{2,0},{4,6},{6,4},{8,10},{10,8},{12,14},{14,12},{16,18},{18,... | collective-permute-start | bytes 2359304 | tf_op jit(solution)/shard_map/ppermute | solution.py:17
  50.5 16.1 %collective-permute-start.12 = (bf16[384,512]{1,0:T(8,128)(2,1)S(1)}, bf16[384,512]{1,0:T(8,128)(2,1)S(1)}, u32[]{:S(2)}, u32[]{:S(2)}) collective-permute-start(bf16[384,512]{1,0:T(8,128)(2,1)S(1)} %collective-permute-done.11), channel_id=1, source_target_pairs={{0,1},{1,0},{2,3},{3,2},{4,5},{5,4},{6,7},{7,6},{8,9},{9,8},{10,11... | collective-permute-start | bytes 1179656 | tf_op jit(solution)/shard_map/ppermute | solution.py:17
  53.7 1.2 %copy-start.4 = (bf16[512,1024]{1,0:T(8,128)(2,1)S(1)}, bf16[512,1024]{1,0:T(8,128)(2,1)}, u32[]{:S(2)}) copy-start(bf16[512,1024]{1,0:T(8,128)(2,1)} %param.11) | copy-start | bytes 3145732
  55.0 19.9 %collective-permute-start.14 = (bf16[2,384,512]{2,1,0:T(8,128)(2,1)S(1)}, bf16[2,384,512]{2,1,0:T(8,128)(2,1)S(1)}, u32[]{:S(2)}, u32[]{:S(2)}) collective-permute-start(bf16[2,384,512]{2,1,0:T(8,128)(2,1)S(1)} %fusion.32.near_ref), channel_id=1, source_target_pairs={{0,4},{2,6},{4,0},{6,2},{8,12},{10,14},{12,8},{14,10},{16,20},{18,... | collective-permute-start | bytes 2359304 | tf_op jit(solution)/shard_map/ppermute | solution.py:17
  55.6 19.3 %collective-permute-start.13 = (bf16[2,384,512]{2,1,0:T(8,128)(2,1)S(1)}, bf16[2,384,512]{2,1,0:T(8,128)(2,1)S(1)}, u32[]{:S(2)}, u32[]{:S(2)}) collective-permute-start(bf16[2,384,512]{2,1,0:T(8,128)(2,1)S(1)} %fusion.32.near_ref), channel_id=1, source_target_pairs={{0,8},{2,10},{4,12},{6,14},{8,0},{10,2},{12,4},{14,6},{16,24},{18,... | collective-permute-start | bytes 2359304 | tf_op jit(solution)/shard_map/ppermute | solution.py:17
  58.2 15.4 %collective-permute-start.7 = (bf16[256,1024]{1,0:T(8,128)(2,1)S(1)}, bf16[256,1024]{1,0:T(8,128)(2,1)S(1)}, u32[]{:S(2)}, u32[]{:S(2)}) collective-permute-start(bf16[256,1024]{1,0:T(8,128)(2,1)S(1)} %slice_select_fusion), channel_id=1, source_target_pairs={{0,1},{1,0},{2,3},{3,2},{4,5},{5,4},{6,7},{7,6},{8,9},{9,8},{10,11... | collective-permute-start | bytes 1572872 | tf_op jit(solution)/shard_map/ppermute | solution.py:17
  66.6 18.4 %collective-permute-start.6 = (bf16[384,512]{1,0:T(8,128)(2,1)S(1)}, bf16[384,512]{1,0:T(8,128)(2,1)S(1)}, u32[]{:S(2)}, u32[]{:S(2)}) collective-permute-start(bf16[384,512]{1,0:T(8,128)(2,1)S(1)} %attention.2), channel_id=1, source_target_pairs={{0,1},{1,0},{2,3},{3,2},{4,5},{5,4},{6,7},{7,6},{8,9},{9,8},{10,11... | collective-permute-start | bytes 1179656 | tf_op jit(solution)/shard_map/ppermute | solution.py:17
  73.6 11.2 %collective-permute-start.8 = (bf16[256,1024]{1,0:T(8,128)(2,1)S(1)}, bf16[256,1024]{1,0:T(8,128)(2,1)S(1)}, u32[]{:S(2)}, u32[]{:S(2)}) collective-permute-start(bf16[256,1024]{1,0:T(8,128)(2,1)S(1)} %collective-permute-done.7), channel_id=1, source_target_pairs={{0,2},{2,0},{4,6},{6,4},{8,10},{10,8},{12,14},{14,12},{16,18},{18,... | collective-permute-start | bytes 1572872 | tf_op jit(solution)/shard_map/ppermute | solution.py:17
  83.0 12.0 %collective-permute-start.16 = (bf16[384,512]{1,0:T(8,128)(2,1)S(1)}, bf16[384,512]{1,0:T(8,128)(2,1)S(1)}, u32[]{:S(2)}, u32[]{:S(2)}) collective-permute-start(bf16[384,512]{1,0:T(8,128)(2,1)S(1)} %attention.3), channel_id=1, source_target_pairs={{0,1},{1,0},{2,3},{3,2},{4,5},{5,4},{6,7},{7,6},{8,9},{9,8},{10,11... | collective-permute-start | bytes 1179656 | tf_op jit(solution)/shard_map/ppermute | solution.py:17
  88.2 1.9 %copy-start.5 = (bf16[1536,1024]{1,0:T(8,128)(2,1)S(1)}, bf16[1536,1024]{1,0:T(8,128)(2,1)}, u32[]{:S(2)}) copy-start(bf16[1536,1024]{1,0:T(8,128)(2,1)} %param.13) | copy-start | bytes 9437188
  90.9 12.5 %collective-permute-start.9 = (bf16[384,512]{1,0:T(8,128)(2,1)S(1)}, bf16[384,512]{1,0:T(8,128)(2,1)S(1)}, u32[]{:S(2)}, u32[]{:S(2)}) collective-permute-start(bf16[384,512]{1,0:T(8,128)(2,1)S(1)} %fusion.18), channel_id=1, source_target_pairs={{0,1},{1,0},{2,3},{3,2},{4,5},{5,4},{6,7},{7,6},{8,9},{9,8},{10,11... | collective-permute-start | bytes 1179656 | tf_op jit(solution)/shard_map/ppermute | solution.py:17
  99.1 12.3 %collective-permute-start.17 = (bf16[384,512]{1,0:T(8,128)(2,1)S(1)}, bf16[384,512]{1,0:T(8,128)(2,1)S(1)}, u32[]{:S(2)}, u32[]{:S(2)}) collective-permute-start(bf16[384,512]{1,0:T(8,128)(2,1)S(1)} %fusion.50), channel_id=1, source_target_pairs={{0,1},{1,0},{2,3},{3,2},{4,5},{5,4},{6,7},{7,6},{8,9},{9,8},{10,11... | collective-permute-start | bytes 1179656 | tf_op jit(solution)/shard_map/ppermute | solution.py:17
